TPU v7x, 32 devices: a whole 2x2x4 slice. The times are simulated.
32 devices in a mesh: seq: 16 (over z, y, core), ch: 2 (over x).
Axes of the slice: x: 2, y: 2, z: 4, core: 2. Of those that a mesh axis runs over, the one named last changes fastest.
Arguments:
- value_stream: bfloat16 [4096, 4096], P('seq', 'ch'), may hold values from -6 to 6
- first_gate: bfloat16 [4096, 4096], P('seq', 'ch'), may hold values from -6 to 6
- second_gate: bfloat16 [4096, 4096], P('seq', 'ch'), may hold values from -6 to 6
- first_filter: bfloat16 [4096, 4096], P('seq', 'ch'), may hold values from -1 to 1
- second_filter: bfloat16 [4096, 4096], P('seq', 'ch'), may hold values from -1 to 1
- first_skip: float32 [4096], P('ch'), may hold values from -1 to 1
- second_skip: float32 [4096], P('ch'), may hold values from -1 to 1
- out_weight: bfloat16 [4096, 4096], P('ch'), may hold values from -0.09375 to 0.09375
Outputs:
- output: bfloat16 [4096, 4096], P('seq', 'ch')
All inputs are finite; a program needn't handle non-finite values.
Results may differ from a plain program's by a relative error of at most 0.019.
Values may be sent and summed in bfloat16 or wider, within the bound.
A program may use at most 128 MiB of HBM per device.

v0:
```python
import math

import jax
import jax.numpy as jnp
from jax import lax
from jax.sharding import PartitionSpec as P

ROWS = 4
INNER = 64


def rotation(first_index, second_index, period):
    phase_angle = (first_index * second_index % period).astype(jnp.float32) * (
        2.0 * math.pi / period
    )
    return (jnp.cos(phase_angle), -jnp.sin(phase_angle))


def spread(twisted):
    return lax.all_to_all(twisted, "seq", split_axis=1, concat_axis=2, tiled=True)


def forward(signal, tables):
    coarse_real, coarse_imag, inner_real, inner_imag, twist_real, twist_imag = tables[:6]
    half_rows, inner_part, channels = signal.shape
    folded = signal.reshape(half_rows, inner_part * channels)
    part_real = jnp.dot(coarse_real, folded, preferred_element_type=jnp.float32).reshape(
        -1, inner_part, channels
    )
    part_imag = jnp.dot(coarse_imag, folded, preferred_element_type=jnp.float32).reshape(
        -1, inner_part, channels
    )
    turn_real = twist_real[:, :, None]
    turn_imag = twist_imag[:, :, None]
    twisted = jnp.stack(
        [
            (part_real * turn_real - part_imag * turn_imag).astype(jnp.bfloat16),
            (part_real * turn_imag + part_imag * turn_real).astype(jnp.bfloat16),
        ]
    )
    arrived = spread(twisted)
    spec_real = jnp.einsum(
        "db,cbk->cdk", inner_real, arrived[0], preferred_element_type=jnp.float32
    ) - jnp.einsum("db,cbk->cdk", inner_imag, arrived[1], preferred_element_type=jnp.float32)
    spec_imag = jnp.einsum(
        "db,cbk->cdk", inner_real, arrived[1], preferred_element_type=jnp.float32
    ) + jnp.einsum("db,cbk->cdk", inner_imag, arrived[0], preferred_element_type=jnp.float32)
    return (spec_real, spec_imag)


def multiply(signal_spec, filter_spec):
    prod_real = (signal_spec[0] * filter_spec[0] - signal_spec[1] * filter_spec[1]).astype(
        jnp.bfloat16
    )
    prod_imag = (signal_spec[0] * filter_spec[1] + signal_spec[1] * filter_spec[0]).astype(
        jnp.bfloat16
    )
    return (prod_real, prod_imag)


def inverse(product, tables, points):
    inner_real, inner_imag = (tables[2], tables[3])
    untwist_real, untwist_imag, lifted_real, lifted_imag = tables[6:10]
    prod_real, prod_imag = product
    sum_real = jnp.einsum(
        "bd,cdk->bck", inner_real, prod_real, preferred_element_type=jnp.float32
    ) + jnp.einsum("bd,cdk->bck", inner_imag, prod_imag, preferred_element_type=jnp.float32)
    sum_imag = jnp.einsum(
        "bd,cdk->bck", inner_real, prod_imag, preferred_element_type=jnp.float32
    ) - jnp.einsum("bd,cdk->bck", inner_imag, prod_real, preferred_element_type=jnp.float32)
    turn_real = untwist_real[:, :, None]
    turn_imag = untwist_imag[:, :, None]
    twisted = jnp.stack(
        [
            (sum_real * turn_real + sum_imag * turn_imag).astype(jnp.bfloat16),
            (sum_imag * turn_real - sum_real * turn_imag).astype(jnp.bfloat16),
        ]
    )
    arrived = spread(twisted)
    summed = jnp.einsum(
        "ac,bck->abk", lifted_real, arrived[0], preferred_element_type=jnp.float32
    ) + jnp.einsum("ac,bck->abk", lifted_imag, arrived[1], preferred_element_type=jnp.float32)
    return summed / points


def shards(
    value_stream,
    first_gate,
    second_gate,
    first_filter,
    second_filter,
    first_skip,
    second_skip,
    out_weight,
):
    seq_count = lax.axis_size("seq")
    position = lax.axis_index("seq")
    tok_rows, channels = value_stream.shape
    coarse_len = 2 * ROWS * seq_count
    points = coarse_len * INNER
    coarse_rows = jnp.arange(coarse_len, dtype=jnp.int32)[:, None]
    coarse_real, coarse_imag = rotation(
        coarse_rows, jnp.arange(coarse_len // 2, dtype=jnp.int32)[None, :], coarse_len
    )
    inner_index = jnp.arange(INNER, dtype=jnp.int32)
    inner_real, inner_imag = rotation(inner_index[:, None], inner_index[None, :], INNER)
    inner_part = INNER // seq_count
    coarse_part = coarse_len // seq_count
    lifted_real, lifted_imag = rotation(
        jnp.arange(coarse_len // 2, dtype=jnp.int32)[:, None], coarse_rows.T, coarse_len
    )
    own_inner = position * inner_part + jnp.arange(inner_part, dtype=jnp.int32)[None, :]
    twist_real, twist_imag = rotation(coarse_rows, own_inner, points)
    own_coarse = position * coarse_part + jnp.arange(coarse_part, dtype=jnp.int32)[None, :]
    untwist_real, untwist_imag = rotation(inner_index[:, None], own_coarse, points)
    tables = (
        coarse_real.astype(jnp.bfloat16),
        coarse_imag.astype(jnp.bfloat16),
        inner_real.astype(jnp.bfloat16),
        inner_imag.astype(jnp.bfloat16),
        twist_real,
        twist_imag,
        untwist_real,
        untwist_imag,
        lifted_real.astype(jnp.bfloat16),
        lifted_imag.astype(jnp.bfloat16),
    )
    grid_shape = (ROWS, INNER, channels)
    value_cols, filter_one, filter_two, gate_one, gate_two = (
        lax.all_to_all(
            value_stream.reshape(grid_shape), "seq", split_axis=1, concat_axis=0, tiled=True
        ),
        lax.all_to_all(
            first_filter.reshape(grid_shape), "seq", split_axis=1, concat_axis=0, tiled=True
        ),
        lax.all_to_all(
            second_filter.reshape(grid_shape), "seq", split_axis=1, concat_axis=0, tiled=True
        ),
        lax.all_to_all(
            first_gate.reshape(grid_shape), "seq", split_axis=1, concat_axis=0, tiled=True
        ),
        lax.all_to_all(
            second_gate.reshape(grid_shape), "seq", split_axis=1, concat_axis=0, tiled=True
        ),
    )
    spec_one = forward(filter_one, tables)
    spec_two = forward(filter_two, tables)
    conv_one = inverse(multiply(forward(value_cols, tables), spec_one), tables, points)
    first_mixed = (
        gate_one.astype(jnp.float32) * (conv_one + first_skip * value_cols.astype(jnp.float32))
    ).astype(jnp.bfloat16)
    conv_two = inverse(multiply(forward(first_mixed, tables), spec_two), tables, points)
    second_mixed = (
        gate_two.astype(jnp.float32) * (conv_two + second_skip * first_mixed.astype(jnp.float32))
    ).astype(jnp.bfloat16)
    rows_mixed = lax.all_to_all(
        second_mixed, "seq", split_axis=0, concat_axis=1, tiled=True
    ).reshape(tok_rows, channels)
    partial_terms = jnp.dot(rows_mixed, out_weight, preferred_element_type=jnp.float32)
    return lax.psum_scatter(
        partial_terms.astype(jnp.bfloat16), "ch", scatter_dimension=1, tiled=True
    )


def solution(mesh):
    return jax.shard_map(
        shards,
        mesh=mesh,
        in_specs=(
            P("seq", "ch"),
            P("seq", "ch"),
            P("seq", "ch"),
            P("seq", "ch"),
            P("seq", "ch"),
            P("ch"),
            P("ch"),
            P("ch", None),
        ),
        out_specs=P("seq", "ch"),
        check_vma=False,
    )
```

profile of v0, /device:TPU:5, one launch (start us, length us, event | category | flops | bytes accessed | tf_op | source)
XLA Modules:
  0.0 874.3 jit_solution(4806053082908689317)
XLA Ops:
  9.7 6.7 all-to-all-start.8
  18.2 21.6 %all-to-all-done.8 = bf16[4,64,2048]{2,0,1:T(4,128)(2,1)S(1)} async-done(((bf16[4,64,2048]{2,0,1:T(4,128)(2,1)}), bf16[4,64,2048]{2,0,1:T(4,128)(2,1)S(1)}, u32[]{:S(2)}, u32[]{:S(2)}) %all-to-all-start.8) | async-done | bytes 1048608 | tf_op jit(solution)/shard_map/all_to_all | solution.py:136
  39.8 6.4 all-to-all-start.4
  48.0 21.7 %all-to-all-done.4 = bf16[4,64,2048]{2,0,1:T(4,128)(2,1)S(1)} async-done(((bf16[4,64,2048]{2,0,1:T(4,128)(2,1)}), bf16[4,64,2048]{2,0,1:T(4,128)(2,1)S(1)}, u32[]{:S(2)}, u32[]{:S(2)}) %all-to-all-start.4) | async-done | bytes 1048608 | tf_op jit(solution)/shard_map/all_to_all | solution.py:133
  69.6 6.8 all-to-all-start.2
  93.3 6.5 all-to-all-done.2
  104.3 10.1 %fusion.18 = (bf16[1,128,4,2048]{3,1,2,0:T(8,128)(2,1)}, bf16[1,128,4,2048]{3,1,2,0:T(8,128)(2,1)}, bf16[1,128,4,2048]{3,1,2,0:T(8,128)(2,1)S(1)}, bf16[1,128,4,...) fusion(f32[128,4,2048]{2,0,1:T(8,128)S(1)} %copy-done.6, ...), kind=kOutput, calls=%fused_computation.61 | convolution fusion | flops 159506432 | bytes 34607104 | tf_op jit(solution)/shard_map/dot_general | solution.py:27
  116.4 5.3 copy.166
  121.7 6.4 all-to-all-start.5
  130.0 5.2 copy.160
  135.2 75.4 %all-to-all-done.5 = bf16[2,128,4,2048]{3,2,0,1:T(4,128)(2,1)} async-done(((bf16[2,128,4,2048]{3,2,0,1:T(4,128)(2,1)}), bf16[2,128,4,2048]{3,2,0,1:T(4,128)(2,1)}, u32[]{:S(2)}, u32[]{:S(2)}) %all-to-all-start.5) | async-done | bytes 4194336 | tf_op jit(solution)/shard_map/all_to_all | solution.py:20
  210.6 15.1 %all-to-all-start.3 = ((bf16[2,128,4,2048]{3,2,0,1:T(4,128)(2,1)}), bf16[2,128,4,2048]{3,2,0,1:T(4,128)(2,1)}, u32[]{:S(2)}, u32[]{:S(2)}) async-start(bf16[2,128,4,2048]{3,2,0,1:T(4,128)(2,1)} %copy.160), calls=%async_computation.3 | async-start | bytes 8388608 | tf_op jit(solution)/shard_map/all_to_all | solution.py:20
  227.7 4.3 copy.268
  250.1 58.1 %all-to-all-done.3 = bf16[2,128,4,2048]{3,2,0,1:T(4,128)(2,1)} async-done(((bf16[2,128,4,2048]{3,2,0,1:T(4,128)(2,1)}), bf16[2,128,4,2048]{3,2,0,1:T(4,128)(2,1)}, u32[]{:S(2)}, u32[]{:S(2)}) %all-to-all-start.3) | async-done | bytes 4194336 | tf_op jit(solution)/shard_map/all_to_all | solution.py:20
  308.2 15.0 %all-to-all-start.1 = ((bf16[4,64,2048]{2,0,1:T(4,128)(2,1)}), bf16[4,64,2048]{2,0,1:T(4,128)(2,1)S(1)}, u32[]{:S(2)}, u32[]{:S(2)}) async-start(bf16[4,64,2048]{2,0,1:T(4,128)(2,1)} %copy.153), calls=%async_computation.1 | async-start | bytes 2097152 | tf_op jit(solution)/shard_map/all_to_all | solution.py:139
  323.2 4.3 copy.269
  352.8 4.3 copy.168
  357.1 6.2 all-to-all-start.6
  365.2 5.2 copy.181
  370.5 75.4 %all-to-all-done.6 = bf16[2,64,8,2048]{3,2,0,1:T(8,128)(2,1)} async-done(((bf16[2,64,8,2048]{3,2,0,1:T(8,128)(2,1)}), bf16[2,64,8,2048]{3,2,0,1:T(8,128)(2,1)}, u32[]{:S(2)}, u32[]{:S(2)}) %all-to-all-start.6) | async-done | bytes 4194336 | tf_op jit(solution)/shard_map/all_to_all | solution.py:20
  445.9 15.4 %all-to-all-start.9 = ((bf16[2,128,4,2048]{3,2,0,1:T(4,128)(2,1)}), bf16[2,128,4,2048]{3,2,0,1:T(4,128)(2,1)}, u32[]{:S(2)}, u32[]{:S(2)}) async-start(bf16[2,128,4,2048]{3,2,0,1:T(4,128)(2,1)} %copy.181), calls=%async_computation.9 | async-start | bytes 8388608 | tf_op jit(solution)/shard_map/all_to_all | solution.py:20
  475.8 5.2 copy.175
  480.9 62.8 %all-to-all-done.9 = bf16[2,128,4,2048]{3,2,0,1:T(4,128)(2,1)} async-done(((bf16[2,128,4,2048]{3,2,0,1:T(4,128)(2,1)}), bf16[2,128,4,2048]{3,2,0,1:T(4,128)(2,1)}, u32[]{:S(2)}, u32[]{:S(2)}) %all-to-all-start.9) | async-done | bytes 4194336 | tf_op jit(solution)/shard_map/all_to_all | solution.py:20
  543.7 15.1 %all-to-all-start.7 = ((bf16[2,128,4,2048]{3,2,0,1:T(4,128)(2,1)}), bf16[2,128,4,2048]{3,2,0,1:T(4,128)(2,1)}, u32[]{:S(2)}, u32[]{:S(2)}) async-start(bf16[2,128,4,2048]{3,2,0,1:T(4,128)(2,1)} %copy.175), calls=%async_computation.7 | async-start | bytes 8388608 | tf_op jit(solution)/shard_map/all_to_all | solution.py:20
  582.7 58.5 %all-to-all-done.7 = bf16[2,128,4,2048]{3,2,0,1:T(4,128)(2,1)} async-done(((bf16[2,128,4,2048]{3,2,0,1:T(4,128)(2,1)}), bf16[2,128,4,2048]{3,2,0,1:T(4,128)(2,1)}, u32[]{:S(2)}, u32[]{:S(2)}) %all-to-all-start.7) | async-done | bytes 4194336 | tf_op jit(solution)/shard_map/all_to_all | solution.py:20
  641.2 15.1 %all-to-all-start = ((bf16[4,64,2048]{2,0,1:T(4,128)(2,1)}), bf16[4,64,2048]{2,0,1:T(4,128)(2,1)}, u32[]{:S(2)}, u32[]{:S(2)}) async-start(bf16[4,64,2048]{2,0,1:T(4,128)(2,1)} %copy.151), calls=%async_computation | async-start | bytes 2097152 | tf_op jit(solution)/shard_map/all_to_all | solution.py:142
  686.0 4.3 copy.183
  690.3 6.0 all-to-all-start.10
  701.2 77.7 %all-to-all-done.10 = bf16[2,64,8,2048]{3,2,0,1:T(8,128)(2,1)} async-done(((bf16[2,64,8,2048]{3,2,0,1:T(8,128)(2,1)}), bf16[2,64,8,2048]{3,2,0,1:T(8,128)(2,1)}, u32[]{:S(2)}, u32[]{:S(2)}) %all-to-all-start.10) | async-done | bytes 4194336 | tf_op jit(solution)/shard_map/all_to_all | solution.py:20
  784.0 39.4 %all_to_all.168 = bf16[64,4,2048]{2,1,0:T(4,128)(2,1)S(1)} all-to-all(bf16[64,4,2048]{2,1,0:T(4,128)(2,1)S(1)} %copy.185), channel_id=1, replica_groups=mesh['seq'=16,'ch'=2] {'seq'}, dimensions={0} | all-to-all | bytes 2097152 | tf_op jit(solution)/shard_map/all_to_all | solution.py:156
  824.1 11.5 %convolution_convert_fusion = bf16[256,4096]{1,0:T(8,128)(2,1)} fusion(bf16[256,2048]{1,0:T(8,128)(2,1)S(1)} %reshape.209, bf16[2048,4096]{1,0:T(8,128)(2,1)} %param.15), kind=kOutput, calls=%fused_computation | convolution fusion | flops 4296015872 | bytes 19922944 | tf_op jit(solution)/shard_map/dot_general | solution.py:159
  835.6 31.6 %reduce-scatter.2.cloned.1.call-done = bf16[256,2048]{1,0:T(8,128)(2,1)} async-done(((bf16[256,4096]{1,0:T(8,128)(2,1)}), bf16[256,2048]{1,0:T(8,128)(2,1)}) %reduce-scatter.2.cloned.1.call-update) | async-done | bytes 1048592 | tf_op jit(solution)/shard_map/reduce_scatter | solution.py:160
  (132 shorter events, 158.0 us)
Async XLA Ops:
  6.5 9.8 %copy-start.18 = (bf16[256,2048]{1,0:T(8,128)(2,1)S(1)}, bf16[256,2048]{1,0:T(8,128)(2,1)}, u32[]{:S(2)}) copy-start(bf16[256,2048]{1,0:T(8,128)(2,1)} %param.11) | copy-start | bytes 3145732
  6.5 39.6 %copy-start.19 = (bf16[256,2048]{1,0:T(8,128)(2,1)S(1)}, bf16[256,2048]{1,0:T(8,128)(2,1)}, u32[]{:S(2)}) copy-start(bf16[256,2048]{1,0:T(8,128)(2,1)} %param.8) | copy-start | bytes 3145732
  9.7 30.1 %all-to-all-start.8 = ((bf16[4,64,2048]{2,0,1:T(4,128)(2,1)}), bf16[4,64,2048]{2,0,1:T(4,128)(2,1)S(1)}, u32[]{:S(2)}, u32[]{:S(2)}) async-start(bf16[4,64,2048]{2,0,1:T(4,128)(2,1)} %copy.177), calls=%async_computation.8 | async-start | bytes 2097152 | tf_op jit(solution)/shard_map/all_to_all | solution.py:136
  39.8 29.8 %all-to-all-start.4 = ((bf16[4,64,2048]{2,0,1:T(4,128)(2,1)}), bf16[4,64,2048]{2,0,1:T(4,128)(2,1)S(1)}, u32[]{:S(2)}, u32[]{:S(2)}) async-start(bf16[4,64,2048]{2,0,1:T(4,128)(2,1)} %copy.162), calls=%async_computation.4 | async-start | bytes 2097152 | tf_op jit(solution)/shard_map/all_to_all | solution.py:133
  69.6 30.1 %all-to-all-start.2 = ((bf16[4,64,2048]{2,0,1:T(4,128)(2,1)}), bf16[4,64,2048]{2,0,1:T(4,128)(2,1)S(1)}, u32[]{:S(2)}, u32[]{:S(2)}) async-start(bf16[4,64,2048]{2,0,1:T(4,128)(2,1)} %copy.155), calls=%async_computation.2 | async-start | bytes 2097152 | tf_op jit(solution)/shard_map/all_to_all | solution.py:130
  99.7 4.6 copy-start.7
  101.7 2.6 copy-start.6
  121.7 89.0 %all-to-all-start.5 = ((bf16[2,128,4,2048]{3,2,0,1:T(4,128)(2,1)}), bf16[2,128,4,2048]{3,2,0,1:T(4,128)(2,1)}, u32[]{:S(2)}, u32[]{:S(2)}) async-start(bf16[2,128,4,2048]{3,2,0,1:T(4,128)(2,1)} %copy.166), calls=%async_computation.5 | async-start | bytes 8388608 | tf_op jit(solution)/shard_map/all_to_all | solution.py:20
  135.2 90.5 %copy-start.20 = (bf16[256,2048]{1,0:T(8,128)(2,1)S(1)}, bf16[256,2048]{1,0:T(8,128)(2,1)}, u32[]{:S(2)}) copy-start(bf16[256,2048]{1,0:T(8,128)(2,1)} %param.9) | copy-start | bytes 3145732
  210.6 97.5 %all-to-all-start.3 = ((bf16[2,128,4,2048]{3,2,0,1:T(4,128)(2,1)}), bf16[2,128,4,2048]{3,2,0,1:T(4,128)(2,1)}, u32[]{:S(2)}, u32[]{:S(2)}) async-start(bf16[2,128,4,2048]{3,2,0,1:T(4,128)(2,1)} %copy.160), calls=%async_computation.3 | async-start | bytes 8388608 | tf_op jit(solution)/shard_map/all_to_all | solution.py:20
  308.2 48.9 %all-to-all-start.1 = ((bf16[4,64,2048]{2,0,1:T(4,128)(2,1)}), bf16[4,64,2048]{2,0,1:T(4,128)(2,1)S(1)}, u32[]{:S(2)}, u32[]{:S(2)}) async-start(bf16[4,64,2048]{2,0,1:T(4,128)(2,1)} %copy.153), calls=%async_computation.1 | async-start | bytes 2097152 | tf_op jit(solution)/shard_map/all_to_all | solution.py:139
  333.4 2.8 copy-start.2
  338.7 2.2 copy-start.8
  340.9 1.6 copy-start.3
  340.9 2.8 copy-start.10
  340.9 4.0 copy-start.12
  357.1 6.2 copy-start.15
  357.1 88.8 %all-to-all-start.6 = ((bf16[2,64,8,2048]{3,2,0,1:T(8,128)(2,1)}), bf16[2,64,8,2048]{3,2,0,1:T(8,128)(2,1)}, u32[]{:S(2)}, u32[]{:S(2)}) async-start(bf16[2,64,8,2048]{3,2,0,1:T(8,128)(2,1)} %copy.168), calls=%async_computation.6 | async-start | bytes 8388608 | tf_op jit(solution)/shard_map/all_to_all | solution.py:20
  370.5 90.8 %copy-start.14 = (f32[16,4,4,2048]{3,0,2,1:T(8,128)S(1)}, f32[16,4,4,2048]{3,0,2,1:T(8,128)}, u32[]{:S(2)}) copy-start(f32[16,4,4,2048]{3,0,2,1:T(8,128)} %get-tuple-element.29) | copy-start | bytes 6291460
  445.9 97.8 %all-to-all-start.9 = ((bf16[2,128,4,2048]{3,2,0,1:T(4,128)(2,1)}), bf16[2,128,4,2048]{3,2,0,1:T(4,128)(2,1)}, u32[]{:S(2)}, u32[]{:S(2)}) async-start(bf16[2,128,4,2048]{3,2,0,1:T(4,128)(2,1)} %copy.181), calls=%async_computation.9 | async-start | bytes 8388608 | tf_op jit(solution)/shard_map/all_to_all | solution.py:20
  466.0 3.1 copy-start.23
  468.5 1.6 copy-start.16
  468.5 2.2 copy-start.17
  480.9 77.9 %copy-start.21 = (bf16[256,2048]{1,0:T(8,128)(2,1)S(1)}, bf16[256,2048]{1,0:T(8,128)(2,1)}, u32[]{:S(2)}) copy-start(bf16[256,2048]{1,0:T(8,128)(2,1)} %param.10) | copy-start | bytes 3145732
  543.7 97.5 %all-to-all-start.7 = ((bf16[2,128,4,2048]{3,2,0,1:T(4,128)(2,1)}), bf16[2,128,4,2048]{3,2,0,1:T(4,128)(2,1)}, u32[]{:S(2)}, u32[]{:S(2)}) async-start(bf16[2,128,4,2048]{3,2,0,1:T(4,128)(2,1)} %copy.175), calls=%async_computation.7 | async-start | bytes 8388608 | tf_op jit(solution)/shard_map/all_to_all | solution.py:20
  641.2 49.1 %all-to-all-start = ((bf16[4,64,2048]{2,0,1:T(4,128)(2,1)}), bf16[4,64,2048]{2,0,1:T(4,128)(2,1)}, u32[]{:S(2)}, u32[]{:S(2)}) async-start(bf16[4,64,2048]{2,0,1:T(4,128)(2,1)} %copy.151), calls=%async_computation | async-start | bytes 2097152 | tf_op jit(solution)/shard_map/all_to_all | solution.py:142
  666.5 2.9 copy-start.4
  671.9 2.2 copy-start.9
  674.1 2.8 copy-start.11
  674.1 4.0 copy-start.13
  690.3 88.6 %all-to-all-start.10 = ((bf16[2,64,8,2048]{3,2,0,1:T(8,128)(2,1)}), bf16[2,64,8,2048]{3,2,0,1:T(8,128)(2,1)}, u32[]{:S(2)}, u32[]{:S(2)}) async-start(bf16[2,64,8,2048]{3,2,0,1:T(8,128)(2,1)} %copy.183), calls=%async_computation.10 | async-start | bytes 8388608 | tf_op jit(solution)/shard_map/all_to_all | solution.py:20
  696.3 170.9 %reduce-scatter.2.cloned.1.call-start = ((), (), s32[]{:S(2)}) async-start(), calls=%async_computation.13 | async-start | bytes 3145728 | tf_op jit(solution)/shard_map/reduce_scatter | solution.py:160
  (4 other events, 5.5 us)
Sparse Core Ops, SparseCore 0:
  835.7 31.3 reduce-scatter.1
where the time goes:
time: 881 us; the launch traced here: 874 us
  waiting for transfers between devices  489 us (56%)
  local copies, waits for them, and re-layouts  123 us (14%)
  starting transfers between devices  114 us (13%)
  matrix products  83.5 us (9%)
  blocking collectives  39.4 us (4%)
  between operations  14.2 us (2%)
  other arithmetic  11 us (1%)
    all_to_all x6, waiting for transfers between devices, spread(): lax.all_to_all(twisted, 'seq', split_axis=1, concat_axis=2, tiled=True)  408 us
    all_to_all x6, starting transfers between devices, spread(): lax.all_to_all(twisted, 'seq', split_axis=1, concat_axis=2, tiled=True)  64.1 us
    all_to_all x1, blocking collectives, shards(): lax.all_to_all(second_mixed, 'seq', split_axis=0, concat_axis=1, tiled=True)  39.4 us
    reduce_scatter x1, waiting for transfers between devices, shards(): lax.psum_scatter(partial_terms.astype(jnp.bfloat16), 'ch', scatter_dimens...  31.6 us
    all_to_all x6, local copies, waits for them, and re-layouts, spread(): lax.all_to_all(twisted, 'seq', split_axis=1, concat_axis=2, tiled=True)  22 us
    all_to_all x1, waiting for transfers between devices, shards(): lax.all_to_all(first_filter.reshape(grid_shape), 'seq', split_axis=1, con...  21.7 us
    all_to_all x1, waiting for transfers between devices, shards(): lax.all_to_all(second_filter.reshape(grid_shape), 'seq', split_axis=1, co...  21.6 us
    another operation x4, local copies, waits for them, and re-layouts, forward(): jnp.stack([(part_real * turn_real - part_imag * turn_imag).astype(jnp.bfl...  20.9 us
  transfers between devices with their start and end apart: 12, of which 10 were waited for; matrix products, arithmetic and copies ran while one was open for 19% of the time, Pallas kernels for 0%

commit v1 on v0

v1 whole, which is shorter than its diff:
```python
import math

import jax
import jax.numpy as jnp
from jax import lax
from jax.sharding import PartitionSpec as P

INNER = 64


def rotation(first_index, second_index, period):
    phase_angle = (first_index * second_index % period).astype(jnp.float32) * (
        2.0 * math.pi / period
    )
    return (jnp.cos(phase_angle), -jnp.sin(phase_angle))


def make_tables(tokens):
    points = 2 * tokens
    coarse_len = points // INNER
    coarse = jnp.arange(coarse_len, dtype=jnp.int32)
    inner = jnp.arange(INNER, dtype=jnp.int32)
    coarse_real, coarse_imag = rotation(coarse[:, None], coarse[None, : coarse_len // 2], coarse_len)
    inner_real, inner_imag = rotation(inner[:, None], inner[None, :], INNER)
    twist_real, twist_imag = rotation(coarse[:, None], inner[None, :], points)
    outer = jnp.concatenate([coarse_real, coarse_imag], 0).astype(jnp.bfloat16)
    inside = jnp.concatenate(
        [
            jnp.concatenate([inner_real, -inner_imag], 1),
            jnp.concatenate([inner_imag, inner_real], 1),
        ],
        0,
    ).astype(jnp.bfloat16)
    return outer, inside, twist_real[:, :, None], twist_imag[:, :, None]


def forward(signal, tables):
    outer, inside, twist_real, twist_imag = tables
    tokens, channels = signal.shape
    part = jnp.dot(
        outer, signal.reshape(tokens // INNER, INNER * channels), preferred_element_type=jnp.float32
    ).reshape(2, -1, INNER, channels)
    twisted = jnp.concatenate(
        [
            (part[0] * twist_real - part[1] * twist_imag).astype(jnp.bfloat16),
            (part[0] * twist_imag + part[1] * twist_real).astype(jnp.bfloat16),
        ],
        axis=1,
    )
    spec = jnp.einsum("pq,cqk->cpk", inside, twisted, preferred_element_type=jnp.float32)
    return spec[:, :INNER], spec[:, INNER:]


def convolve(signal_spec, filter_spec, tables):
    outer, inside, twist_real, twist_imag = tables
    product = jnp.concatenate(
        [
            (signal_spec[0] * filter_spec[0] - signal_spec[1] * filter_spec[1]).astype(jnp.bfloat16),
            (signal_spec[0] * filter_spec[1] + signal_spec[1] * filter_spec[0]).astype(jnp.bfloat16),
        ],
        axis=1,
    )
    back = jnp.einsum("qp,cqk->cpk", inside, product, preferred_element_type=jnp.float32)
    back_real, back_imag = back[:, :INNER], back[:, INNER:]
    coarse_len, _, channels = back_real.shape
    turned = jnp.stack(
        [
            (back_real * twist_real + back_imag * twist_imag).astype(jnp.bfloat16),
            (back_imag * twist_real - back_real * twist_imag).astype(jnp.bfloat16),
        ]
    ).reshape(2 * coarse_len, INNER * channels)
    summed = lax.dot_general(
        outer, turned, (((0,), (0,)), ((), ())), preferred_element_type=jnp.float32
    )
    return (summed / (coarse_len * INNER)).reshape(-1, channels)


def shards(
    value_stream,
    first_gate,
    second_gate,
    first_filter,
    second_filter,
    first_skip,
    second_skip,
    out_weight,
):
    seq_count = lax.axis_size("seq")
    position = lax.axis_index("seq")
    tok_rows, channels = value_stream.shape
    share = channels // seq_count
    tables = make_tables(tok_rows * seq_count)

    def own_channels(field):
        return lax.all_to_all(field, "seq", split_axis=1, concat_axis=0, tiled=True)

    skip_one = lax.dynamic_slice_in_dim(first_skip, position * share, share)
    skip_two = lax.dynamic_slice_in_dim(second_skip, position * share, share)
    filter_one = own_channels(first_filter)
    value = own_channels(value_stream)
    gate_one = own_channels(first_gate)
    filter_two = own_channels(second_filter)
    conv_one = convolve(forward(value, tables), forward(filter_one, tables), tables)
    first_mixed = (
        gate_one.astype(jnp.float32) * (conv_one + skip_one * value.astype(jnp.float32))
    ).astype(jnp.bfloat16)
    conv_two = convolve(forward(first_mixed, tables), forward(filter_two, tables), tables)
    mixed = (conv_two + skip_two * first_mixed.astype(jnp.float32)).astype(jnp.bfloat16)
    rows = lax.all_to_all(mixed, "seq", split_axis=0, concat_axis=1, tiled=True)
    rows_mixed = (second_gate.astype(jnp.float32) * rows.astype(jnp.float32)).astype(jnp.bfloat16)
    partial_terms = jnp.dot(rows_mixed, out_weight, preferred_element_type=jnp.float32)
    return lax.psum_scatter(
        partial_terms.astype(jnp.bfloat16), "ch", scatter_dimension=1, tiled=True
    )


def solution(mesh):
    return jax.shard_map(
        shards,
        mesh=mesh,
        in_specs=(
            P("seq", "ch"),
            P("seq", "ch"),
            P("seq", "ch"),
            P("seq", "ch"),
            P("seq", "ch"),
            P("ch"),
            P("ch"),
            P("ch", None),
        ),
        out_specs=P("seq", "ch"),
        check_vma=False,
    )
```

time: 881 us -> 255 us (0.29)
  waiting for transfers between devices: 489 us -> 76.8 us
  starting transfers between devices: 114 us -> 26 us
  local copies, waits for them, and re-layouts: 123 us -> 43 us
  matrix products: 83.5 us -> 33.7 us
  other arithmetic: 11 us -> 28.4 us
    all_to_all x11 -> x4, waiting for transfers between devices: 458 us -> 45.2 us  [own_channels(): return lax.all_to_all(field, 'seq', split_axis=1, concat_axis=0, tiled=True)]
    all_to_all x11 -> x4, starting transfers between devices: 114 us -> 25.8 us  [own_channels(): return lax.all_to_all(field, 'seq', split_axis=1, concat_axis=0, tiled=True)]
    dot_general x36 -> x12, matrix products: 72 us -> 22.2 us  [the longest x4 6.93 us: forward(): jnp.dot(outer, signal.reshape(tokens // INNER, INNER * channels), preferr...]
    another operation x6 -> x0, local copies, waits for them, and re-layouts: 29.5 us -> none  [the longest x4 20.9 us: forward(): jnp.stack([(part_real * turn_real - part_imag * turn_imag).astype(jnp.bfl...]
    squeeze x8 -> x0, local copies, waits for them, and re-layouts: 23.2 us -> none  [the longest x4 13 us: forward(): arrived[0]]
    all_to_all x10 -> x4, local copies, waits for them, and re-layouts: 25.1 us -> 7.44 us  [own_channels(): return lax.all_to_all(field, 'seq', split_axis=1, concat_axis=0, tiled=True)]
    convert_element_type x2 -> x5, other arithmetic: 3.44 us -> 19.3 us  [the longest x2 12.1 us: forward(): (part[0] * twist_real - part[1] * twist_imag).astype(jnp.bfloat16)]
    slice x4 -> x0, local copies, waits for them, and re-layouts: 13.5 us -> none  [forward(): arrived[0]]
  transfers between devices with their start and end apart: 12 -> 5, of which waited for: 10 -> 4; matrix products, arithmetic and copies ran while one was open for 19% -> 23% of each run, Pallas kernels for 0% -> 0%
where the time goes in v1:
time: 255 us; the launch traced here: 252 us
  waiting for transfers between devices  76.8 us (30%)
  local copies, waits for them, and re-layouts  43 us (17%)
  matrix products  33.7 us (13%)
  blocking collectives  30.6 us (12%)
  other arithmetic  28.4 us (11%)
  starting transfers between devices  26 us (10%)
  between operations  13.7 us (5%)
    all_to_all x4, waiting for transfers between devices, own_channels(): return lax.all_to_all(field, 'seq', split_axis=1, concat_axis=0, tiled=True)  45.2 us
    reduce_scatter x1, waiting for transfers between devices, shards(): lax.psum_scatter(partial_terms.astype(jnp.bfloat16), 'ch', scatter_dimens...  31.6 us
    all_to_all x1, blocking collectives, shards(): rows = lax.all_to_all(mixed, 'seq', split_axis=0, concat_axis=1, tiled=True)  30.6 us
    all_to_all x4, starting transfers between devices, own_channels(): return lax.all_to_all(field, 'seq', split_axis=1, concat_axis=0, tiled=True)  25.8 us
    unnamed x30, local copies, waits for them, and re-layouts  25.4 us
    convert_element_type x2, other arithmetic, forward(): (part[0] * twist_real - part[1] * twist_imag).astype(jnp.bfloat16)  12.1 us
    dot_general x1, matrix products, shards(): jnp.dot(rows_mixed, out_weight, preferred_element_type=jnp.float32)  11.5 us
    another operation x4, other arithmetic, convolve(): jnp.stack([(back_real * twist_real + back_imag * twist_imag).astype(jnp.b...  8.01 us
  transfers between devices with their start and end apart: 5, of which 4 were waited for; matrix products, arithmetic and copies ran while one was open for 23% of the time, Pallas kernels for 0%

profile of v1, /device:TPU:5, one launch (start us, length us, event | category | flops | bytes accessed | tf_op | source)
XLA Modules:
  0.0 252.3 jit_solution(14157239907145584466)
XLA Ops:
  9.0 6.7 %all-to-all-start.1 = ((bf16[256,16,128]{2,0,1:T(8,128)(2,1)}), bf16[256,16,128]{2,0,1:T(8,128)(2,1)S(1)}, u32[]{:S(2)}, u32[]{:S(2)}) async-start(bf16[256,16,128]{2,0,1:T(8,128)(2,1)} %copy_bitcast_fusion.2), calls=%async_computation.1 | async-start | bytes 2097152 | tf_op jit(solution)/shard_map/all_to_all | solution.py:95
  16.9 22.2 %all-to-all-done.1 = bf16[256,16,128]{2,0,1:T(8,128)(2,1)S(1)} async-done(((bf16[256,16,128]{2,0,1:T(8,128)(2,1)}), bf16[256,16,128]{2,0,1:T(8,128)(2,1)S(1)}, u32[]{:S(2)}, u32[]{:S(2)}) %all-to-all-start.1) | async-done | bytes 1048608 | tf_op jit(solution)/shard_map/all_to_all | solution.py:95
  39.1 6.4 %all-to-all-start.2 = ((bf16[256,16,128]{2,0,1:T(8,128)(2,1)}), bf16[256,16,128]{2,0,1:T(8,128)(2,1)S(1)}, u32[]{:S(2)}, u32[]{:S(2)}) async-start(bf16[256,16,128]{2,0,1:T(8,128)(2,1)} %copy_bitcast_fusion.1), calls=%async_computation.2 | async-start | bytes 2097152 | tf_op jit(solution)/shard_map/all_to_all | solution.py:95
  48.1 2.5 copy_bitcast_fusion.3
  50.6 2.5 copy_bitcast_fusion
  53.6 15.3 %all-to-all-done.2 = bf16[256,16,128]{2,0,1:T(8,128)(2,1)S(1)} async-done(((bf16[256,16,128]{2,0,1:T(8,128)(2,1)}), bf16[256,16,128]{2,0,1:T(8,128)(2,1)S(1)}, u32[]{:S(2)}, u32[]{:S(2)}) %all-to-all-start.2) | async-done | bytes 1048608 | tf_op jit(solution)/shard_map/all_to_all | solution.py:95
  68.9 6.4 %all-to-all-start = ((bf16[256,16,128]{2,0,1:T(8,128)(2,1)}), bf16[256,16,128]{2,0,1:T(8,128)(2,1)S(1)}, u32[]{:S(2)}, u32[]{:S(2)}) async-start(bf16[256,16,128]{2,0,1:T(8,128)(2,1)} %copy_bitcast_fusion.3), calls=%async_computation | async-start | bytes 2097152 | tf_op jit(solution)/shard_map/all_to_all | solution.py:95
  77.5 2.8 %copy.39 = f32[16,8,64,128]{3,2,1,0:T(8,128)} copy(f32[16,8,64,128]{3,1,2,0:T(8,128)S(1)} %get-tuple-element.23) | data formatting | bytes 8388608
  80.3 2.7 %copy.40 = f32[16,8,64,128]{3,2,1,0:T(8,128)} copy(f32[16,8,64,128]{3,1,2,0:T(8,128)S(1)} %get-tuple-element.24) | data formatting | bytes 8388608
  85.6 2.7 %copy.41 = f32[16,8,64,128]{3,2,1,0:T(8,128)} copy(f32[16,8,64,128]{3,1,2,0:T(8,128)S(1)} %get-tuple-element.25) | data formatting | bytes 8388608
  88.3 2.7 %copy.42 = f32[16,8,64,128]{3,2,1,0:T(8,128)} copy(f32[16,8,64,128]{3,1,2,0:T(8,128)S(1)} %get-tuple-element.26) | data formatting | bytes 8388608
  91.0 7.7 %all-to-all-done = bf16[256,16,128]{2,0,1:T(8,128)(2,1)S(1)} async-done(((bf16[256,16,128]{2,0,1:T(8,128)(2,1)}), bf16[256,16,128]{2,0,1:T(8,128)(2,1)S(1)}, u32[]{:S(2)}, u32[]{:S(2)}) %all-to-all-start) | async-done | bytes 1048608 | tf_op jit(solution)/shard_map/all_to_all | solution.py:95
  98.7 6.4 %all-to-all-start.3 = ((bf16[256,16,128]{2,0,1:T(8,128)(2,1)}), bf16[256,16,128]{2,0,1:T(8,128)(2,1)}, u32[]{:S(2)}, u32[]{:S(2)}) async-start(bf16[256,16,128]{2,0,1:T(8,128)(2,1)} %copy_bitcast_fusion), calls=%async_computation.3 | async-start | bytes 2097152 | tf_op jit(solution)/shard_map/all_to_all | solution.py:95
  105.5 1.5 reshape.125
  107.1 7.9 %fusion.17 = (bf16[128,64,128]{2,1,0:T(8,128)(2,1)S(1)}, bf16[128,64,128]{2,1,0:T(8,128)(2,1)S(1)}, bf16[128,64,128]{2,1,0:T(8,128)(2,1)S(1)}, bf16[128,64,128]{2,1,0:T(8,128)(2,1)S(1)}) fusion(f32[16,8,64,128]{3,2,1,0:T(8,128)} %copy.40, f32[16,8,64,128]{3,2,1,0:T(8,128)} %copy.39, f32[128,64]{1,0:T(8,128)S(1)} %copy.24, f32[128,64]{1,0:T(8,128)S(1)} %copy.23, ...), kind=kLoop, calls=%fused_computation.34 | loop fusion | flops 16777216 | bytes 25231360 | tf_op jit(solution)/shard_map/convert_element_type | solution.py:45
  117.8 2.2 subtract_convert_fusion.3
  121.5 3.6 %fusion.62 = (bf16[1,128,64,128]{3,2,1,0:T(8,128)(2,1)S(1)}, bf16[1,128,64,128]{3,2,1,0:T(8,128)(2,1)S(1)}) fusion(f32[128,128,128]{2,1,0:T(8,128)S(1)} %fusion.53, f32[128,64]{1,0:T(8,128)S(1)} %copy.24, f32[128,64]{1,0:T(8,128)S(1)} %copy.23), kind=kLoop, calls=%fused_computation.87 | loop fusion | flops 8388608 | bytes 12648448 | tf_op jit(solution)/shard_map/stack | solution.py:66
  125.6 2.6 %convolution_multiply_fusion.1 = f32[64,8192]{1,0:T(8,128)S(1)} fusion(bf16[32,8,64,128]{3,2,1,0:T(8,128)(2,1)S(1)} %bitcast.174, bf16[128,64]{0,1:T(8,128)(2,1)S(1)} %get-tuple-element.34, bf16[128,64]{0,1:T(8,128)(2,1)S(1)} %get-tuple-element.33), kind=kOutput, calls=%fused_computation.1 | convolution fusion | flops 269025280 | bytes 6324224 | tf_op jit(solution)/shard_map/dot_general | solution.py:72
  128.2 1.5 reshape.124
  129.7 3.1 %fusion.67 = f32[256,8192]{1,0:T(8,128)S(1)} fusion(f32[64,8192]{1,0:T(8,128)} %reshape.125, f32[64,8192]{1,0:T(8,128)S(1)} %convolution_multiply_fusion.1, bf16[64,8192]{1,0:T(8,128)(2,1)} %copy-done.6, f32[8192]{0:T(1024)S(1)} %broadcast_bitcast_fusion, bf16[128,64]{0,1:T(8,128)(2,1)S(1)} %get-tuple-element.34, bf16[128,64]{0,1:T(8,128)(2,1)S(1)} %get-tuple-element.33), kind=kOutput, calls=%fused_computation.98 | convolution fusion | flops 271122432 | bytes 13697024 | tf_op jit(solution)/shard_map/dot_general | solution.py:40
  133.7 2.8 %copy.44 = f32[16,8,64,128]{3,2,1,0:T(8,128)} copy(f32[16,8,64,128]{3,1,2,0:T(8,128)S(1)} %get-tuple-element.21) | data formatting | bytes 8388608
  136.5 2.7 %copy.45 = f32[16,8,64,128]{3,2,1,0:T(8,128)} copy(f32[16,8,64,128]{3,1,2,0:T(8,128)S(1)} %get-tuple-element.22) | data formatting | bytes 8388608
  139.2 1.7 reshape.121
  147.3 4.3 %fusion.7 = (bf16[128,64,128]{2,1,0:T(8,128)(2,1)S(1)}, bf16[128,64,128]{2,1,0:T(8,128)(2,1)S(1)}, bf16[128,64,128]{2,1,0:T(8,128)(2,1)S(1)}, bf16[128,64,128]{2,1,0:T(8,128)(2,1)S(1)}) fusion(f32[16,8,64,128]{3,2,1,0:T(8,128)S(1)} %copy-done.3, f32[16,8,64,128]{3,2,1,0:T(8,128)S(1)} %copy-done.2, f32[128,64]{1,0:T(8,128)S(1)} %copy.24, ...), kind=kLoop, calls=%fused_computation.16 | loop fusion | flops 16777216 | bytes 25231360 | tf_op jit(solution)/shard_map/convert_element_type | solution.py:45
  154.5 2.2 subtract_convert_fusion.1
  158.2 3.6 %fusion.64 = (bf16[1,128,64,128]{3,2,1,0:T(8,128)(2,1)S(1)}, bf16[1,128,64,128]{3,2,1,0:T(8,128)(2,1)S(1)}) fusion(f32[128,128,128]{2,1,0:T(8,128)S(1)} %fusion.44, f32[128,64]{1,0:T(8,128)S(1)} %copy.24, f32[128,64]{1,0:T(8,128)S(1)} %copy.23), kind=kLoop, calls=%fused_computation.89 | loop fusion | flops 8388608 | bytes 12648448 | tf_op jit(solution)/shard_map/stack | solution.py:66
  162.2 3.9 %convolution_multiply_fusion = f32[64,8192]{1,0:T(8,128)} fusion(bf16[32,8,64,128]{3,2,1,0:T(8,128)(2,1)S(1)} %bitcast.173, bf16[128,64]{0,1:T(8,128)(2,1)S(1)} %get-tuple-element.34, bf16[128,64]{0,1:T(8,128)(2,1)S(1)} %get-tuple-element.33), kind=kOutput, calls=%fused_computation | convolution fusion | flops 269025280 | bytes 6324224 | tf_op jit(solution)/shard_map/dot_general | solution.py:72
  166.1 2.7 %reshape.123 = f32[16,256,128]{2,1,0:T(8,128)} reshape(f32[64,8192]{1,0:T(8,128)} %convolution_multiply_fusion) | data formatting | bytes 4194304 | tf_op jit(solution)/shard_map/reshape | solution.py:75
  168.9 2.9 %add_convert_fusion.4 = bf16[16,256,128]{2,1,0:T(8,128)(2,1)S(1)} fusion(f32[16,256,128]{2,1,0:T(8,128)} %reshape.123, f32[16,256,128]{2,1,0:T(8,128)} %reshape.124, f32[128]{0:T(128)S(1)} %dynamic_slice.6, f32[128]{0:T(128)S(1)} %dynamic_slice.7, bf16[256,16,128]{2,0,1:T(8,128)(2,1)S(1)} %all-to-all-done, bf16[256,16,128]{2,0,1:T(8,128)(2,1)S(1)} %copy-done.5), kind=kLoop, calls=%fused_computation.95 | loop fusion | flops 5242880 | bytes 7341056 | tf_op jit(solution)/shard_map/convert_element_type | solution.py:108
  171.8 30.6 %all_to_all.71 = bf16[16,256,128]{2,1,0:T(8,128)(2,1)S(1)} all-to-all(bf16[16,256,128]{2,1,0:T(8,128)(2,1)S(1)} %add_convert_fusion.4), channel_id=1, replica_groups=mesh['seq'=16,'ch'=2] {'seq'}, dimensions={0} | all-to-all | bytes 2097152 | tf_op jit(solution)/shard_map/all_to_all | solution.py:109
  202.4 11.5 %convolution_convert_fusion = bf16[256,4096]{1,0:T(8,128)(2,1)} fusion(bf16[2048,4096]{1,0:T(8,128)(2,1)} %param.15, bf16[256,2048]{1,0:T(8,128)(2,1)S(1)} %copy-done.8, bf16[16,256,128]{2,1,0:T(8,128)(2,1)S(1)} %all_to_all.71), kind=kOutput, calls=%fused_computation.2 | convolution fusion | flops 4298113024 | bytes 20971520 | tf_op jit(solution)/shard_map/dot_general | solution.py:111
  213.9 31.6 %reduce-scatter.2.cloned.1.call-done = bf16[256,2048]{1,0:T(8,128)(2,1)} async-done(((bf16[256,4096]{1,0:T(8,128)(2,1)}), bf16[256,2048]{1,0:T(8,128)(2,1)}) %reduce-scatter.2.cloned.1.call-update) | async-done | bytes 1048592 | tf_op jit(solution)/shard_map/reduce_scatter | solution.py:112
  (55 shorter events, 28.9 us)
Async XLA Ops:
  6.5 1.2 copy-start
  6.5 9.1 %copy-start.7 = (bf16[256,2048]{1,0:T(8,128)(2,1)S(1)}, bf16[256,2048]{1,0:T(8,128)(2,1)}, u32[]{:S(2)}) copy-start(bf16[256,2048]{1,0:T(8,128)(2,1)} %param.11) | copy-start | bytes 3145732
  9.0 30.1 %all-to-all-start.1 = ((bf16[256,16,128]{2,0,1:T(8,128)(2,1)}), bf16[256,16,128]{2,0,1:T(8,128)(2,1)S(1)}, u32[]{:S(2)}, u32[]{:S(2)}) async-start(bf16[256,16,128]{2,0,1:T(8,128)(2,1)} %copy_bitcast_fusion.2), calls=%async_computation.1 | async-start | bytes 2097152 | tf_op jit(solution)/shard_map/all_to_all | solution.py:95
  39.1 14.5 %copy-start.4 = (bf16[256,16,128]{2,0,1:T(8,128)(2,1)}, bf16[256,16,128]{2,0,1:T(8,128)(2,1)S(1)}, u32[]{:S(2)}) copy-start(bf16[256,16,128]{2,0,1:T(8,128)(2,1)S(1)} %all-to-all-done.1) | copy-start | bytes 3145732
  39.1 29.8 %all-to-all-start.2 = ((bf16[256,16,128]{2,0,1:T(8,128)(2,1)}), bf16[256,16,128]{2,0,1:T(8,128)(2,1)S(1)}, u32[]{:S(2)}, u32[]{:S(2)}) async-start(bf16[256,16,128]{2,0,1:T(8,128)(2,1)} %copy_bitcast_fusion.1), calls=%async_computation.2 | async-start | bytes 2097152 | tf_op jit(solution)/shard_map/all_to_all | solution.py:95
  53.6 23.0 %copy-start.6 = (bf16[64,8192]{1,0:T(8,128)(2,1)}, bf16[64,8192]{1,0:T(8,128)(2,1)S(1)}, u32[]{:S(2)}) copy-start(bf16[64,8192]{1,0:T(8,128)(2,1)S(1)} %reshape.118) | copy-start | bytes 3145732
  68.9 29.8 %all-to-all-start = ((bf16[256,16,128]{2,0,1:T(8,128)(2,1)}), bf16[256,16,128]{2,0,1:T(8,128)(2,1)S(1)}, u32[]{:S(2)}, u32[]{:S(2)}) async-start(bf16[256,16,128]{2,0,1:T(8,128)(2,1)} %copy_bitcast_fusion.3), calls=%async_computation | async-start | bytes 2097152 | tf_op jit(solution)/shard_map/all_to_all | solution.py:95
  98.7 40.5 %all-to-all-start.3 = ((bf16[256,16,128]{2,0,1:T(8,128)(2,1)}), bf16[256,16,128]{2,0,1:T(8,128)(2,1)}, u32[]{:S(2)}, u32[]{:S(2)}) async-start(bf16[256,16,128]{2,0,1:T(8,128)(2,1)} %copy_bitcast_fusion), calls=%async_computation.3 | async-start | bytes 2097152 | tf_op jit(solution)/shard_map/all_to_all | solution.py:95
  105.1 140.4 %reduce-scatter.2.cloned.1.call-start = ((), (), s32[]{:S(2)}) async-start(), calls=%async_computation.6 | async-start | bytes 3145728 | tf_op jit(solution)/shard_map/reduce_scatter | solution.py:112
  143.9 2.2 copy-start.2
  143.9 3.5 %copy-start.3 = (f32[16,8,64,128]{3,2,1,0:T(8,128)S(1)}, f32[16,8,64,128]{3,2,1,0:T(8,128)}, u32[]{:S(2)}) copy-start(f32[16,8,64,128]{3,2,1,0:T(8,128)} %copy.45) | copy-start | bytes 12582916
  162.2 6.7 %copy-start.5 = (bf16[256,16,128]{2,0,1:T(8,128)(2,1)S(1)}, bf16[256,16,128]{2,0,1:T(8,128)(2,1)}, u32[]{:S(2)}) copy-start(bf16[256,16,128]{2,0,1:T(8,128)(2,1)} %copy-done.4) | copy-start | bytes 3145732
  168.9 33.5 %copy-start.8 = (bf16[256,2048]{1,0:T(8,128)(2,1)S(1)}, bf16[256,2048]{1,0:T(8,128)(2,1)}, u32[]{:S(2)}) copy-start(bf16[256,2048]{1,0:T(8,128)(2,1)} %param.10) | copy-start | bytes 3145732
  202.4 43.1 %copy-start.1 = (bf16[256,2048]{1,0:T(8,128)(2,1)S(1)}, bf16[256,2048]{1,0:T(8,128)(2,1)}, u32[]{:S(2)}) copy-start(bf16[256,2048]{1,0:T(8,128)(2,1)} %param.8) | copy-start | bytes 3145732
Sparse Core Ops, SparseCore 0:
  214.1 31.3 reduce-scatter.1

commit v2 on v1

--- a/solution.py
+++ b/solution.py
@@ -2,7 +2,11 @@
 
 import jax
 import jax.numpy as jnp
+import ml_dtypes
+import numpy as np
 from jax import lax
+from jax.experimental import pallas as pl
+from jax.experimental.pallas import tpu as pltpu
 from jax.sharding import PartitionSpec as P
 
 INNER = 64
@@ -73,6 +77,126 @@
         outer, turned, (((0,), (0,)), ((), ())), preferred_element_type=jnp.float32
     )
     return (summed / (coarse_len * INNER)).reshape(-1, channels)
+
+
+def folded_tables(tokens):
+    points = 2 * tokens
+    coarse_len = points // INNER
+    half = coarse_len // 2
+    kept = half + 8
+    b = np.arange(INNER)[:, None, None, None]
+    c = np.arange(kept)[None, :, None, None]
+    a = np.arange(half)[None, None, None, :]
+    angle = (c * (INNER * a + b) % points) * (2.0 * math.pi / points)
+    table = np.concatenate([np.cos(angle), -np.sin(angle)], axis=2) * (c <= half)
+    weight = np.where((c == 0) | (c == half), 1.0, 2.0) / points
+    forth = table.reshape(INNER, 2 * kept, half)
+    back = (table * weight).reshape(INNER, 2 * kept, half).transpose(0, 2, 1)
+    index = np.arange(INNER)
+    angle = (index[:, None] * index[None, :] % INNER) * (2.0 * math.pi / INNER)
+    real, imag = np.cos(angle), -np.sin(angle)
+    inside = np.block([[real, -imag], [imag, real]])
+    return tuple(jnp.asarray(t.astype(ml_dtypes.bfloat16)) for t in (forth, back, inside, inside.T))
+
+
+def convolve_rows(signal, taps, forth, back, inside, outside, signal_half, taps_half, total):
+    tokens, channels = signal.shape
+    half = tokens // INNER
+    kept2 = forth.shape[1]
+
+    def outer(b, _):
+        rows = pl.ds(b, half, stride=INNER)
+        both = jnp.concatenate([signal[rows, :], taps[rows, :]], axis=1).astype(jnp.bfloat16)
+        part = jnp.dot(forth[b], both, preferred_element_type=jnp.float32)
+        spread = pl.ds(b, kept2, stride=INNER)
+        signal_half[spread, :] = part[:, :channels]
+        taps_half[spread, :] = part[:, channels:]
+        return 0
+
+    lax.fori_loop(0, INNER, outer, 0, unroll=4)
+
+    def inner(c, _):
+        rows = pl.ds(pl.multiple_of(c * 2 * INNER, 2 * INNER), 2 * INNER)
+        both = jnp.concatenate([signal_half[rows, :], taps_half[rows, :]], axis=1)
+        spec = jnp.dot(inside[...], both.astype(jnp.bfloat16), preferred_element_type=jnp.float32)
+        sig_re, sig_im = spec[:INNER, :channels], spec[INNER:, :channels]
+        tap_re, tap_im = spec[:INNER, channels:], spec[INNER:, channels:]
+        product = jnp.concatenate(
+            [sig_re * tap_re - sig_im * tap_im, sig_re * tap_im + sig_im * tap_re], axis=0
+        ).astype(jnp.bfloat16)
+        signal_half[rows, :] = jnp.dot(outside[...], product, preferred_element_type=jnp.float32)
+        return 0
+
+    lax.fori_loop(0, half + 1, inner, 0, unroll=5)
+
+    def last(b, _):
+        folded = signal_half[pl.ds(b, kept2, stride=INNER), :].astype(jnp.bfloat16)
+        total[pl.ds(b, half, stride=INNER), :] = jnp.dot(
+            back[b], folded, preferred_element_type=jnp.float32
+        )
+        return 0
+
+    lax.fori_loop(0, INNER, last, 0, unroll=4)
+
+
+def first_kernel(
+    taps_ref, value_ref, skip_ref, forth, back, inside, outside, out_ref,
+    signal, taps, signal_half, taps_half,
+):
+    signal[...] = value_ref[...].astype(jnp.float32)
+    taps[...] = taps_ref[...].astype(jnp.float32)
+    convolve_rows(signal, taps, forth, back, inside, outside, signal_half, taps_half, out_ref)
+    out_ref[...] += skip_ref[...] * signal[...]
+
+
+def second_kernel(
+    taps_ref, first_ref, gate_ref, skip_ref, forth, back, inside, outside, out_ref,
+    signal, taps, signal_half, taps_half, total,
+):
+    mixed = (gate_ref[...].astype(jnp.float32) * first_ref[...]).astype(jnp.bfloat16)
+    signal[...] = mixed.astype(jnp.float32)
+    taps[...] = taps_ref[...].astype(jnp.float32)
+    convolve_rows(signal, taps, forth, back, inside, outside, signal_half, taps_half, total)
+    out_ref[...] = (total[...] + skip_ref[...] * signal[...]).astype(jnp.bfloat16)
+
+
+def call_local(kernel, dtype, tokens, channels, extra, *operands):
+    kept2 = operands[-4].shape[1]
+    field = pltpu.VMEM((tokens, channels), jnp.float32)
+    half_field = pltpu.VMEM((kept2 * INNER, channels), jnp.float32)
+    return pl.pallas_call(
+        kernel,
+        out_shape=jax.ShapeDtypeStruct((tokens, channels), dtype),
+        in_specs=[pl.BlockSpec(memory_space=pltpu.VMEM)] * len(operands),
+        out_specs=pl.BlockSpec(memory_space=pltpu.VMEM),
+        scratch_shapes=[field, field, half_field, half_field] + [field] * extra,
+        compiler_params=pltpu.CompilerParams(vmem_limit_bytes=48 * 1024 * 1024),
+        cost_estimate=pl.CostEstimate(
+            flops=16_000_000_000, bytes_accessed=8_000_000, transcendentals=0
+        ),
+    )(*operands)
+
+
+def local_mixing(first_filter, value_stream, first_gate, second_filter, skip_one, skip_two):
+    rows, channels = value_stream.shape
+    seq_count = lax.axis_size("seq")
+    tokens, share = rows * seq_count, channels // seq_count
+    tables = folded_tables(tokens)
+
+    def pair(one, two):
+        both = jnp.stack([one, two]).reshape(2, rows, seq_count, share).transpose(2, 0, 1, 3)
+        got = lax.all_to_all(both, "seq", split_axis=0, concat_axis=0, tiled=True)
+        return got[:, 0].reshape(tokens, share), got[:, 1].reshape(tokens, share)
+
+    taps_one, value = pair(first_filter, value_stream)
+    gate_one, taps_two = pair(first_gate, second_filter)
+    first = call_local(
+        first_kernel, jnp.float32, tokens, share, 0, taps_one, value, skip_one[None, :], *tables
+    )
+    return call_local(
+        second_kernel, jnp.bfloat16, tokens, share, 1,
+        taps_two, first, gate_one, skip_two[None, :], *tables,
+    )
 
 
 def shards(
@@ -89,25 +213,39 @@
     position = lax.axis_index("seq")
     tok_rows, channels = value_stream.shape
     share = channels // seq_count
-    tables = make_tables(tok_rows * seq_count)
 
     def own_channels(field):
         return lax.all_to_all(field, "seq", split_axis=1, concat_axis=0, tiled=True)
 
     skip_one = lax.dynamic_slice_in_dim(first_skip, position * share, share)
     skip_two = lax.dynamic_slice_in_dim(second_skip, position * share, share)
-    filter_one = own_channels(first_filter)
-    value = own_channels(value_stream)
-    gate_one = own_channels(first_gate)
-    filter_two = own_channels(second_filter)
-    conv_one = convolve(forward(value, tables), forward(filter_one, tables), tables)
-    first_mixed = (
-        gate_one.astype(jnp.float32) * (conv_one + skip_one * value.astype(jnp.float32))
-    ).astype(jnp.bfloat16)
-    conv_two = convolve(forward(first_mixed, tables), forward(filter_two, tables), tables)
-    mixed = (conv_two + skip_two * first_mixed.astype(jnp.float32)).astype(jnp.bfloat16)
+    if share % 128 == 0:
+        mixed = local_mixing(
+            first_filter, value_stream, first_gate, second_filter, skip_one, skip_two
+        )
+    else:
+        tables = make_tables(tok_rows * seq_count)
+        filter_one = own_channels(first_filter)
+        value = own_channels(value_stream)
+        gate_one = own_channels(first_gate)
+        filter_two = own_channels(second_filter)
+        conv_one = convolve(forward(value, tables), forward(filter_one, tables), tables)
+        first_mixed = (
+            gate_one.astype(jnp.float32) * (conv_one + skip_one * value.astype(jnp.float32))
+        ).astype(jnp.bfloat16)
+        conv_two = convolve(forward(first_mixed, tables), forward(filter_two, tables), tables)
+        mixed = (conv_two + skip_two * first_mixed.astype(jnp.float32)).astype(jnp.bfloat16)
     rows = lax.all_to_all(mixed, "seq", split_axis=0, concat_axis=1, tiled=True)
     rows_mixed = (second_gate.astype(jnp.float32) * rows.astype(jnp.float32)).astype(jnp.bfloat16)
+    if lax.axis_size("ch") == 2:
+        side = lax.axis_index("ch")
+        width = out_weight.shape[1] // 2
+        theirs_weight = lax.dynamic_slice_in_dim(out_weight, (1 - side) * width, width, 1)
+        own_weight = lax.dynamic_slice_in_dim(out_weight, side * width, width, 1)
+        theirs = jnp.dot(rows_mixed, theirs_weight, preferred_element_type=jnp.float32)
+        arrived = lax.ppermute(theirs.astype(jnp.bfloat16), "ch", [(0, 1), (1, 0)])
+        own = jnp.dot(rows_mixed, own_weight, preferred_element_type=jnp.float32)
+        return (own + arrived.astype(jnp.float32)).astype(jnp.bfloat16)
     partial_terms = jnp.dot(rows_mixed, out_weight, preferred_element_type=jnp.float32)
     return lax.psum_scatter(
         partial_terms.astype(jnp.bfloat16), "ch", scatter_dimension=1, tiled=True

time: 255 us -> 216 us (0.85)
  Pallas kernels: 0 us -> 63.5 us
  blocking collectives: 30.6 us -> 0 us
  local copies, waits for them, and re-layouts: 43 us -> 16.3 us
  other arithmetic: 28.4 us -> 4.17 us
  matrix products: 33.7 us -> 13.5 us
  waiting for transfers between devices: 76.8 us -> 90.5 us
  between operations: 13.7 us -> 0.06 us
    pallas_call x0 -> x2, Pallas kernels: none -> 63.5 us  [call_local(): pl.pallas_call(kernel, out_shape=jax.ShapeDtypeStruct((tokens, channels),...]
    reduce_scatter x1 -> x0, waiting for transfers between devices: 31.6 us -> none  [shards(): lax.psum_scatter(partial_terms.astype(jnp.bfloat16), 'ch', scatter_dimens...]
    all_to_all x1 -> x0, blocking collectives: 30.6 us -> none  [shards(): rows = lax.all_to_all(mixed, 'seq', split_axis=0, concat_axis=1, tiled=True)]
    ppermute x0 -> x1, waiting for transfers between devices: none -> 24 us  [shards(): arrived = lax.ppermute(theirs.astype(jnp.bfloat16), 'ch', [(0, 1), (1, 0)])]
    all_to_all x4 -> x3, waiting for transfers between devices: 45.2 us -> 66.5 us  [the longest x2 43.1 us: pair(): got = lax.all_to_all(both, 'seq', split_axis=0, concat_axis=0, tiled=True)]
    dot_general x13 -> x2, matrix products: 33.7 us -> 13.5 us  [the longest x1 6.74 us: shards(): own = jnp.dot(rows_mixed, own_weight, preferred_element_type=jnp.float32)]
    convert_element_type x6 -> x0, other arithmetic: 19.5 us -> none  [the longest x2 12.1 us: forward(): (part[0] * twist_real - part[1] * twist_imag).astype(jnp.bfloat16)]
    unnamed x30 -> x14, local copies, waits for them, and re-layouts: 25.4 us -> 7.25 us
  transfers between devices with their start and end apart: 5 -> 4, of which waited for: 4 -> 4; matrix products, arithmetic and copies ran while one was open for 23% -> 5% of each run, Pallas kernels for 0% -> 15%
where the time goes in v2:
time: 216 us; the launch traced here: 214 us
  waiting for transfers between devices  90.5 us (42%)
  Pallas kernels  63.5 us (29%)
  starting transfers between devices  26.3 us (12%)
  local copies, waits for them, and re-layouts  16.3 us (8%)
  matrix products  13.5 us (6%)
  other arithmetic  4.17 us (2%)
    pallas_call x2, Pallas kernels, call_local(): pl.pallas_call(kernel, out_shape=jax.ShapeDtypeStruct((tokens, channels),...  63.5 us
    all_to_all x2, waiting for transfers between devices, pair(): got = lax.all_to_all(both, 'seq', split_axis=0, concat_axis=0, tiled=True)  43.1 us
    ppermute x1, waiting for transfers between devices, shards(): arrived = lax.ppermute(theirs.astype(jnp.bfloat16), 'ch', [(0, 1), (1, 0)])  24 us
    all_to_all x1, waiting for transfers between devices, shards(): rows = lax.all_to_all(mixed, 'seq', split_axis=0, concat_axis=1, tiled=True)  23.4 us
    all_to_all x2, starting transfers between devices, pair(): got = lax.all_to_all(both, 'seq', split_axis=0, concat_axis=0, tiled=True)  15.8 us
    all_to_all x1, starting transfers between devices, shards(): rows = lax.all_to_all(mixed, 'seq', split_axis=0, concat_axis=1, tiled=True)  9.28 us
    unnamed x14, local copies, waits for them, and re-layouts  7.25 us
    dot_general x1, matrix products, shards(): own = jnp.dot(rows_mixed, own_weight, preferred_element_type=jnp.float32)  6.74 us
  transfers between devices with their start and end apart: 4, of which 4 were waited for; matrix products, arithmetic and copies ran while one was open for 5% of the time, Pallas kernels for 15%

profile of v2, /device:TPU:5, one launch (start us, length us, event | category | flops | bytes accessed | tf_op | source)
XLA Modules:
  0.0 214.3 jit_solution(10868955997384138983)
XLA Ops:
  0.0 0.0 copy-start
  0.0 0.0 copy-start.3
  0.0 1.6 copy.22
  1.6 0.0 copy-done.3
  1.6 1.3 copy.23
  2.9 1.4 maximum_bitcast_fusion.1
  4.3 2.4 %copy.24 = bf16[16,2,256,128]{3,2,1,0:T(8,128)(2,1)} copy(bf16[16,2,256,128]{2,3,0,1:T(8,128)(2,1)S(1)} %maximum_bitcast_fusion.1) | data formatting | bytes 4194304 | tf_op jit(solution)/shard_map/transpose | solution.py:187
  6.7 6.7 %all-to-all-start.1 = ((bf16[16,2,256,128]{3,2,1,0:T(8,128)(2,1)}), bf16[16,2,256,128]{3,2,1,0:T(8,128)(2,1)S(1)}, u32[]{:S(2)}, u32[]{:S(2)}) async-start(bf16[16,2,256,128]{3,2,1,0:T(8,128)(2,1)} %copy.24), calls=%async_computation.1 | async-start | bytes 4194304 | tf_op jit(solution)/shard_map/all_to_all | solution.py:188
  13.4 1.5 copy.19
  14.8 2.3 %copy.20 = bf16[256,2048]{0,1:T(8,128)(2,1)} copy(bf16[256,2048]{1,0:T(8,128)(2,1)} %param.16) | data formatting | bytes 2097152 | tf_op args[4]
  17.1 2.8 %maximum_bitcast_fusion = bf16[16,2,256,128]{2,3,0,1:T(8,128)(2,1)} fusion(bf16[1,256,16,128]{1,3,2,0:T(8,128)(2,1)} %bitcast.37, bf16[1,256,16,128]{1,3,2,0:T(8,128)(2,1)S(1)} %bitcast.36), kind=kLoop, calls=%fused_computation.7 | loop fusion | flops 1048576 | bytes 4194304 | tf_op jit(solution)/shard_map/transpose | solution.py:187
  19.9 3.9 %copy.21 = bf16[16,2,256,128]{3,2,1,0:T(8,128)(2,1)} copy(bf16[16,2,256,128]{2,3,0,1:T(8,128)(2,1)} %maximum_bitcast_fusion) | data formatting | bytes 4194304 | tf_op jit(solution)/shard_map/transpose | solution.py:187
  23.8 32.7 %all-to-all-done.1 = bf16[16,2,256,128]{3,2,1,0:T(8,128)(2,1)S(1)} async-done(((bf16[16,2,256,128]{3,2,1,0:T(8,128)(2,1)}), bf16[16,2,256,128]{3,2,1,0:T(8,128)(2,1)S(1)}, u32[]{:S(2)}, u32[]{:S(2)}) %all-to-all-start.1) | async-done | bytes 2097184 | tf_op jit(solution)/shard_map/all_to_all | solution.py:188
  56.5 9.2 %all-to-all-start = ((bf16[16,2,256,128]{3,2,1,0:T(8,128)(2,1)}), bf16[16,2,256,128]{3,2,1,0:T(8,128)(2,1)}, u32[]{:S(2)}, u32[]{:S(2)}) async-start(bf16[16,2,256,128]{3,2,1,0:T(8,128)(2,1)} %copy.21), calls=%async_computation | async-start | bytes 4194304 | tf_op jit(solution)/shard_map/all_to_all | solution.py:188
  65.7 0.0 copy-done
  65.7 0.1 dynamic-slice_bitcast_fusion.1.skip_ref
  65.8 0.8 dynamic-slice_bitcast_fusion.skip_ref
  66.5 0.0 copy-start.1
  66.5 0.1 fusion.15
  66.7 0.6 copy-done.1
  67.3 0.0 copy-done.2
  67.3 31.3 %shard_map.118.first_ref = f32[4096,128]{1,0:T(8,128)S(1)} custom-call(bf16[4096,128]{1,0:T(8,128)(2,1)S(1)} %bitcast.33, bf16[4096,128]{1,0:T(8,128)(2,1)S(1)} %bitcast.32, f32[1,128]{1,0:T(1,128)S(1)} %dynamic-slice_bitcast_fusion.1.skip_ref, bf16[64,144,64]{2,1,0:T(8,128)(2,1)} %constant.26.clone.forth, bf16[64,64,144]{2,1,0:T(8,128)(2,1)} %constant.27.clone.back, ...), custom_call_target="tpu_custom_call" | custom-call | flops 16000000000 | bytes 8000000 | tf_op jit(solution)/shard_map/pallas_call | solution.py:167
  98.6 10.4 %all-to-all-done = bf16[16,2,256,128]{3,2,1,0:T(8,128)(2,1)} async-done(((bf16[16,2,256,128]{3,2,1,0:T(8,128)(2,1)}), bf16[16,2,256,128]{3,2,1,0:T(8,128)(2,1)}, u32[]{:S(2)}, u32[]{:S(2)}) %all-to-all-start) | async-done | bytes 2097184 | tf_op jit(solution)/shard_map/all_to_all | solution.py:188
  109.0 1.8 fusion.14
  110.7 32.2 %shard_map.119 = bf16[4096,128]{1,0:T(8,128)(2,1)} custom-call(bf16[4096,128]{1,0:T(8,128)(2,1)S(1)} %bitcast.31, f32[4096,128]{1,0:T(8,128)S(1)} %shard_map.118.first_ref, bf16[4096,128]{1,0:T(8,128)(2,1)S(1)} %bitcast.30, f32[1,128]{1,0:T(1,128)S(1)} %dynamic-slice_bitcast_fusion.skip_ref, bf16[64,144,64]{2,1,0:T(8,128)(2,1)} %constant.26.clone.forth, ...), custom_call_target="tpu_custom_call" | custom-call | flops 16000000000 | bytes 8000000 | tf_op jit(solution)/shard_map/pallas_call | solution.py:167
  142.9 9.3 %all-to-all-start.2 = ((bf16[16,256,128]{2,1,0:T(8,128)(2,1)}), bf16[16,256,128]{2,1,0:T(8,128)(2,1)S(1)}, u32[]{:S(2)}, u32[]{:S(2)}) async-start(bf16[16,256,128]{2,1,0:T(8,128)(2,1)} %bitcast.12), calls=%async_computation.2 | async-start | bytes 2097152 | tf_op jit(solution)/shard_map/all_to_all | solution.py:238
  152.2 23.4 %all-to-all-done.2 = bf16[16,256,128]{2,1,0:T(8,128)(2,1)S(1)} async-done(((bf16[16,256,128]{2,1,0:T(8,128)(2,1)}), bf16[16,256,128]{2,1,0:T(8,128)(2,1)S(1)}, u32[]{:S(2)}, u32[]{:S(2)}) %all-to-all-start.2) | async-done | bytes 1048608 | tf_op jit(solution)/shard_map/all_to_all | solution.py:238
  175.7 0.0 copy-done.4
  175.7 6.7 %fusion.4 = bf16[256,2048]{1,0:T(8,128)(2,1)} fusion(bf16[2048,4096]{1,0:T(8,128)(2,1)} %param.19, s32[]{:T(128)S(6)} %select_n.12, bf16[256,2048]{1,0:T(8,128)(2,1)S(1)} %copy-done.4, bf16[16,256,128]{2,1,0:T(8,128)(2,1)S(1)} %all-to-all-done.2), kind=kOutput, calls=%fused_computation.4 | convolution fusion | flops 2150105088 | bytes 11534340 | tf_op jit(solution)/shard_map/dot_general | solution.py:245
  182.4 1.2 collective-permute-start
  183.6 24.0 %collective-permute-done = bf16[256,2048]{1,0:T(8,128)(2,1)S(1)} collective-permute-done((bf16[256,2048]{1,0:T(8,128)(2,1)}, bf16[256,2048]{1,0:T(8,128)(2,1)S(1)}, u32[]{:S(2)}, u32[]{:S(2)}) %collective-permute-start) | collective-permute-done | bytes 1048608 | tf_op jit(solution)/shard_map/ppermute | solution.py:246
  207.6 6.7 %add_convert_fusion = bf16[256,2048]{1,0:T(8,128)(2,1)} fusion(bf16[256,2048]{1,0:T(8,128)(2,1)S(1)} %collective-permute-done, bf16[2048,4096]{1,0:T(8,128)(2,1)} %param.19, s32[]{:T(128)S(6)} %select_n.11, bf16[256,2048]{1,0:T(8,128)(2,1)S(1)} %copy-done.4, bf16[16,256,128]{2,1,0:T(8,128)(2,1)S(1)} %all-to-all-done.2), kind=kOutput, calls=%fused_computation.10 | convolution fusion | flops 2151153664 | bytes 12582916 | tf_op jit(solution)/shard_map/dot_general | solution.py:247
  (2 shorter events, 0.0 us)
Async XLA Ops:
  0.0 65.7 %copy-start = (f32[2048]{0:T(1024)S(1)}, f32[2048]{0:T(1024)}, u32[]{:S(2)}) copy-start(f32[2048]{0:T(1024)} %param.17) | copy-start | bytes 24580
  0.0 1.6 copy-start.3
  6.7 49.8 %all-to-all-start.1 = ((bf16[16,2,256,128]{3,2,1,0:T(8,128)(2,1)}), bf16[16,2,256,128]{3,2,1,0:T(8,128)(2,1)S(1)}, u32[]{:S(2)}, u32[]{:S(2)}) async-start(bf16[16,2,256,128]{3,2,1,0:T(8,128)(2,1)} %copy.24), calls=%async_computation.1 | async-start | bytes 4194304 | tf_op jit(solution)/shard_map/all_to_all | solution.py:188
  56.5 52.4 %all-to-all-start = ((bf16[16,2,256,128]{3,2,1,0:T(8,128)(2,1)}), bf16[16,2,256,128]{3,2,1,0:T(8,128)(2,1)}, u32[]{:S(2)}, u32[]{:S(2)}) async-start(bf16[16,2,256,128]{3,2,1,0:T(8,128)(2,1)} %copy.21), calls=%async_computation | async-start | bytes 4194304 | tf_op jit(solution)/shard_map/all_to_all | solution.py:188
  66.5 0.8 copy-start.1
  66.5 0.8 copy-start.2
  142.9 32.7 %copy-start.4 = (bf16[256,2048]{1,0:T(8,128)(2,1)S(1)}, bf16[256,2048]{1,0:T(8,128)(2,1)}, u32[]{:S(2)}) copy-start(bf16[256,2048]{1,0:T(8,128)(2,1)} %param.14) | copy-start | bytes 3145732
  142.9 32.7 %all-to-all-start.2 = ((bf16[16,256,128]{2,1,0:T(8,128)(2,1)}), bf16[16,256,128]{2,1,0:T(8,128)(2,1)S(1)}, u32[]{:S(2)}, u32[]{:S(2)}) async-start(bf16[16,256,128]{2,1,0:T(8,128)(2,1)} %bitcast.12), calls=%async_computation.2 | async-start | bytes 2097152 | tf_op jit(solution)/shard_map/all_to_all | solution.py:238
  182.4 25.2 %collective-permute-start = (bf16[256,2048]{1,0:T(8,128)(2,1)}, bf16[256,2048]{1,0:T(8,128)(2,1)S(1)}, u32[]{:S(2)}, u32[]{:S(2)}) collective-permute-start(bf16[256,2048]{1,0:T(8,128)(2,1)} %fusion.4), channel_id=1, source_target_pairs={{0,1},{1,0},{2,3},{3,2},{4,5},{5,4},{6,7},{7,6},{8,9},{9,8},{10,11... | collective-permute-start | bytes 3145736 | tf_op jit(solution)/shard_map/ppermute | solution.py:246

commit v3 on v2

--- a/solution.py
+++ b/solution.py
@@ -1,3 +1,4 @@
+import functools
 import math
 
 import jax
@@ -115,19 +116,28 @@
 
     lax.fori_loop(0, INNER, outer, 0, unroll=4)
 
-    def inner(c, _):
-        rows = pl.ds(pl.multiple_of(c * 2 * INNER, 2 * INNER), 2 * INNER)
-        both = jnp.concatenate([signal_half[rows, :], taps_half[rows, :]], axis=1)
-        spec = jnp.dot(inside[...], both.astype(jnp.bfloat16), preferred_element_type=jnp.float32)
-        sig_re, sig_im = spec[:INNER, :channels], spec[INNER:, :channels]
-        tap_re, tap_im = spec[:INNER, channels:], spec[INNER:, channels:]
+    group = math.gcd(half + 1, 5)
+
+    def inner(g, _):
+        slabs = [
+            pl.ds(pl.multiple_of((g * group + i) * 2 * INNER, 2 * INNER), 2 * INNER)
+            for i in range(group)
+        ]
+        sig = jnp.concatenate([signal_half[rows, :].astype(jnp.bfloat16) for rows in slabs], axis=1)
+        tap = jnp.concatenate([taps_half[rows, :].astype(jnp.bfloat16) for rows in slabs], axis=1)
+        sig = jnp.dot(inside[...], sig, preferred_element_type=jnp.float32)
+        tap = jnp.dot(inside[...], tap, preferred_element_type=jnp.float32)
+        sig_re, sig_im = sig[:INNER], sig[INNER:]
+        tap_re, tap_im = tap[:INNER], tap[INNER:]
         product = jnp.concatenate(
             [sig_re * tap_re - sig_im * tap_im, sig_re * tap_im + sig_im * tap_re], axis=0
         ).astype(jnp.bfloat16)
-        signal_half[rows, :] = jnp.dot(outside[...], product, preferred_element_type=jnp.float32)
-        return 0
-
-    lax.fori_loop(0, half + 1, inner, 0, unroll=5)
+        result = jnp.dot(outside[...], product, preferred_element_type=jnp.float32)
+        for i, rows in enumerate(slabs):
+            signal_half[rows, :] = result[:, i * channels : (i + 1) * channels]
+        return 0
+
+    lax.fori_loop(0, (half + 1) // group, inner, 0)
 
     def last(b, _):
         folded = signal_half[pl.ds(b, kept2, stride=INNER), :].astype(jnp.bfloat16)
@@ -199,6 +209,167 @@
     )
 
 
+CHUNKS = 4
+TILE = 512
+
+
+def tail_kernel(
+    count, mixed_ref, gate_ref, weight_ref, out_ref,
+    rows, gated, weight, theirs, own, arrived,
+    weight_sem, local_sem, send_sem, recv_sem, side_send, side_recv,
+):
+    me, side = lax.axis_index("seq"), lax.axis_index("ch")
+    tok_rows, channels = gate_ref.shape
+    share, piece = channels // count, tok_rows // CHUNKS
+    width = out_ref.shape[1]
+    stride = max(count // 2 - 1, 1)
+
+    def weight_copy(slot, owner):
+        columns = pl.ds(pl.multiple_of(owner * width, width), width)
+        return pltpu.make_async_copy(
+            weight_ref.at[:, columns], weight.at[slot], weight_sem.at[slot]
+        )
+
+    weight_copy(0, 1 - side).start()
+    weight_copy(1, side).start()
+
+    barrier = pltpu.get_barrier_semaphore()
+
+    def greet(j, _):
+        pl.semaphore_signal(barrier, inc=1, device_id=(lax.rem(me + j, count), side))
+        return 0
+
+    lax.fori_loop(1, count, greet, 0)
+    pl.semaphore_signal(barrier, inc=1, device_id=(me, 1 - side))
+    pl.semaphore_wait(barrier, count)
+
+    def columns_of(owner):
+        return pl.ds(pl.multiple_of(owner * share, share), share)
+
+    def row_copy(q, j, target, owner):
+        start = pl.multiple_of(target * tok_rows + q * piece, piece)
+        return pltpu.make_async_remote_copy(
+            src_ref=mixed_ref.at[pl.ds(start, piece), :],
+            dst_ref=rows.at[q, :, columns_of(owner)],
+            send_sem=send_sem.at[q, j],
+            recv_sem=recv_sem.at[q, j],
+            device_id=(target, side),
+        )
+
+    def side_copy(q):
+        return pltpu.make_async_remote_copy(
+            src_ref=theirs.at[q],
+            dst_ref=arrived.at[q],
+            send_sem=side_send.at[q],
+            recv_sem=side_recv.at[q],
+            device_id=(me, 1 - side),
+        )
+
+    def local_copy(q):
+        start = pl.multiple_of(me * tok_rows + q * piece, piece)
+        return pltpu.make_async_copy(
+            mixed_ref.at[pl.ds(start, piece), :], rows.at[q, :, columns_of(me)], local_sem.at[q]
+        )
+
+    def send_chunk(q, _):
+        def send(i, _):
+            j = 1 + lax.rem(stride * (i + 1), count - 1)
+            row_copy(q, j, lax.rem(me + j, count), me).start()
+            return 0
+
+        lax.fori_loop(0, count - 1, send, 0)
+        local_copy(q).start()
+        return 0
+
+    lax.fori_loop(0, CHUNKS, send_chunk, 0)
+    weight_copy(0, 1 - side).wait()
+    weight_copy(1, side).wait()
+
+    def work(q, _):
+        def receive(j, _):
+            row_copy(q, j, lax.rem(me + j, count), lax.rem(me + count - j, count)).wait_recv()
+            return 0
+
+        lax.fori_loop(1, count, receive, 0)
+        local_copy(q).wait()
+        gate_rows = pl.ds(pl.multiple_of(q * piece, piece), piece)
+        gated[...] = (
+            gate_ref[gate_rows, :].astype(jnp.float32) * rows[q].astype(jnp.float32)
+        ).astype(jnp.bfloat16)
+
+        def project(slot, t):
+            columns = pl.ds(pl.multiple_of(t * TILE, TILE), TILE)
+            return columns, jnp.dot(
+                gated[...], weight[slot, :, columns], preferred_element_type=jnp.float32
+            )
+
+        def for_other(t, _):
+            columns, terms = project(0, t)
+            theirs[q, :, columns] = terms.astype(jnp.bfloat16)
+            return 0
+
+        def for_self(t, _):
+            columns, terms = project(1, t)
+            own[q, :, columns] = terms
+            return 0
+
+        lax.fori_loop(0, width // TILE, for_other, 0)
+        side_copy(q).start()
+        lax.fori_loop(0, width // TILE, for_self, 0)
+        return 0
+
+    lax.fori_loop(0, CHUNKS, work, 0)
+
+    def finish(q, _):
+        side_copy(q).wait_recv()
+        out_rows = pl.ds(pl.multiple_of(q * piece, piece), piece)
+        out_ref[out_rows, :] = (own[q] + arrived[q].astype(jnp.float32)).astype(jnp.bfloat16)
+        side_copy(q).wait_send()
+
+        def sent(j, _):
+            row_copy(q, j, lax.rem(me + j, count), me).wait_send()
+            return 0
+
+        lax.fori_loop(1, count, sent, 0)
+        return 0
+
+    lax.fori_loop(0, CHUNKS, finish, 0)
+
+
+def project_rows(mixed, gate, out_weight):
+    count = lax.axis_size("seq")
+    tok_rows, channels = gate.shape
+    piece, width = tok_rows // CHUNKS, out_weight.shape[1] // 2
+    in_vmem = pl.BlockSpec(memory_space=pltpu.VMEM)
+    dma = pltpu.SemaphoreType.DMA
+    return pl.pallas_call(
+        functools.partial(tail_kernel, count),
+        out_shape=jax.ShapeDtypeStruct((tok_rows, width), jnp.bfloat16),
+        in_specs=[in_vmem, in_vmem, pl.BlockSpec(memory_space=pl.ANY)],
+        out_specs=in_vmem,
+        scratch_shapes=[
+            pltpu.VMEM((CHUNKS, piece, channels), jnp.bfloat16),
+            pltpu.VMEM((piece, channels), jnp.bfloat16),
+            pltpu.VMEM((2, channels, width), jnp.bfloat16),
+            pltpu.VMEM((CHUNKS, piece, width), jnp.bfloat16),
+            pltpu.VMEM((CHUNKS, piece, width), jnp.float32),
+            pltpu.VMEM((CHUNKS, piece, width), jnp.bfloat16),
+            dma((2,)),
+            dma((CHUNKS,)),
+            dma((CHUNKS, count)),
+            dma((CHUNKS, count)),
+            dma((CHUNKS,)),
+            dma((CHUNKS,)),
+        ],
+        compiler_params=pltpu.CompilerParams(
+            collective_id=0, has_side_effects=True, vmem_limit_bytes=48 * 1024 * 1024
+        ),
+        cost_estimate=pl.CostEstimate(
+            flops=2 * tok_rows * channels * 2 * width, bytes_accessed=20_000_000, transcendentals=0
+        ),
+    )(mixed, gate, out_weight)
+
+
 def shards(
     value_stream,
     first_gate,
@@ -223,6 +394,8 @@
         mixed = local_mixing(
             first_filter, value_stream, first_gate, second_filter, skip_one, skip_two
         )
+        if lax.axis_size("ch") == 2:
+            return project_rows(mixed, second_gate, out_weight)
     else:
         tables = make_tables(tok_rows * seq_count)
         filter_one = own_channels(first_filter)
@@ -237,15 +410,6 @@
         mixed = (conv_two + skip_two * first_mixed.astype(jnp.float32)).astype(jnp.bfloat16)
     rows = lax.all_to_all(mixed, "seq", split_axis=0, concat_axis=1, tiled=True)
     rows_mixed = (second_gate.astype(jnp.float32) * rows.astype(jnp.float32)).astype(jnp.bfloat16)
-    if lax.axis_size("ch") == 2:
-        side = lax.axis_index("ch")
-        width = out_weight.shape[1] // 2
-        theirs_weight = lax.dynamic_slice_in_dim(out_weight, (1 - side) * width, width, 1)
-        own_weight = lax.dynamic_slice_in_dim(out_weight, side * width, width, 1)
-        theirs = jnp.dot(rows_mixed, theirs_weight, preferred_element_type=jnp.float32)
-        arrived = lax.ppermute(theirs.astype(jnp.bfloat16), "ch", [(0, 1), (1, 0)])
-        own = jnp.dot(rows_mixed, own_weight, preferred_element_type=jnp.float32)
-        return (own + arrived.astype(jnp.float32)).astype(jnp.bfloat16)
     partial_terms = jnp.dot(rows_mixed, out_weight, preferred_element_type=jnp.float32)
     return lax.psum_scatter(
         partial_terms.astype(jnp.bfloat16), "ch", scatter_dimension=1, tiled=True

time: 216 us -> 183 us (0.85)
  waiting for transfers between devices: 90.5 us -> 51 us
  Pallas kernels: 63.5 us -> 94.4 us
  matrix products: 13.5 us -> 0 us
  starting transfers between devices: 26.3 us -> 15.8 us
    pallas_call x0 -> x1, Pallas kernels: none -> 47.5 us  [project_rows(): pl.pallas_call(functools.partial(tail_kernel, count), out_shape=jax.Shape...]
    ppermute x1 -> x0, waiting for transfers between devices: 24 us -> none  [shards(): arrived = lax.ppermute(theirs.astype(jnp.bfloat16), 'ch', [(0, 1), (1, 0)])]
    all_to_all x1 -> x0, waiting for transfers between devices: 23.4 us -> none  [shards(): rows = lax.all_to_all(mixed, 'seq', split_axis=0, concat_axis=1, tiled=True)]
    pallas_call x2, Pallas kernels: 63.5 us -> 46.9 us  [call_local(): pl.pallas_call(kernel, out_shape=jax.ShapeDtypeStruct((tokens, channels),...]
    dot_general x2 -> x0, matrix products: 13.5 us -> none  [the longest x1 6.74 us: shards(): own = jnp.dot(rows_mixed, own_weight, preferred_element_type=jnp.float32)]
    all_to_all x1 -> x0, starting transfers between devices: 9.28 us -> none  [shards(): rows = lax.all_to_all(mixed, 'seq', split_axis=0, concat_axis=1, tiled=True)]
    all_to_all x2, waiting for transfers between devices: 43.1 us -> 51 us  [pair(): got = lax.all_to_all(both, 'seq', split_axis=0, concat_axis=0, tiled=True)]
    unnamed x14 -> x15, local copies, waits for them, and re-layouts: 7.25 us -> 8.23 us
  transfers between devices with their start and end apart: 4 -> 2, of which waited for: 4 -> 2; matrix products, arithmetic and copies ran while one was open for 5% -> 6% of each run, Pallas kernels for 15% -> 13%
where the time goes in v3:
time: 183 us
  Pallas kernels  94.4 us (52%)
  waiting for transfers between devices  51 us (28%)
  local copies, waits for them, and re-layouts  17.3 us (9%)
  starting transfers between devices  15.8 us (9%)
  other arithmetic  4.16 us (2%)
    all_to_all x2, waiting for transfers between devices, pair(): got = lax.all_to_all(both, 'seq', split_axis=0, concat_axis=0, tiled=True)  51 us
    pallas_call x1, Pallas kernels, project_rows(): pl.pallas_call(functools.partial(tail_kernel, count), out_shape=jax.Shape...  47.5 us
    pallas_call x2, Pallas kernels, call_local(): pl.pallas_call(kernel, out_shape=jax.ShapeDtypeStruct((tokens, channels),...  46.9 us
    all_to_all x2, starting transfers between devices, pair(): got = lax.all_to_all(both, 'seq', split_axis=0, concat_axis=0, tiled=True)  15.8 us
    unnamed x15, local copies, waits for them, and re-layouts  8.23 us
    transpose x2, local copies, waits for them, and re-layouts, pair(): jnp.stack([one, two]).reshape(2, rows, seq_count, share)  6.32 us
    transpose x2, other arithmetic, pair(): jnp.stack([one, two]).reshape(2, rows, seq_count, share)  4.16 us
  transfers between devices with their start and end apart: 2, of which 2 were waited for; matrix products, arithmetic and copies ran while one was open for 6% of the time, Pallas kernels for 13%

profile of v3, /device:TPU:5, one launch (start us, length us, event | category | flops | bytes accessed | tf_op | source)
XLA Modules:
  0.0 182.7 jit_solution(8860218482894064720)
XLA Ops:
  0.0 0.0 copy-start
  0.0 0.0 copy-start.4
  0.0 1.6 copy.21
  1.6 0.0 copy-done.4
  1.6 1.3 copy.20
  2.9 1.4 maximum_bitcast_fusion.1
  4.3 2.4 %copy.22 = bf16[16,2,256,128]{3,2,1,0:T(8,128)(2,1)} copy(bf16[16,2,256,128]{2,3,0,1:T(8,128)(2,1)S(1)} %maximum_bitcast_fusion.1) | data formatting | bytes 4194304 | tf_op jit(solution)/shard_map/transpose | solution.py:197
  6.7 6.7 %all-to-all-start.1 = ((bf16[16,2,256,128]{3,2,1,0:T(8,128)(2,1)}), bf16[16,2,256,128]{3,2,1,0:T(8,128)(2,1)S(1)}, u32[]{:S(2)}, u32[]{:S(2)}) async-start(bf16[16,2,256,128]{3,2,1,0:T(8,128)(2,1)} %copy.22), calls=%async_computation.1 | async-start | bytes 4194304 | tf_op jit(solution)/shard_map/all_to_all | solution.py:198
  13.4 1.5 copy.18
  14.8 2.3 %copy.17 = bf16[256,2048]{0,1:T(8,128)(2,1)} copy(bf16[256,2048]{1,0:T(8,128)(2,1)} %param.13) | data formatting | bytes 2097152 | tf_op args[1]
  17.1 2.7 %maximum_bitcast_fusion = bf16[16,2,256,128]{2,3,0,1:T(8,128)(2,1)} fusion(bf16[1,256,16,128]{1,3,2,0:T(8,128)(2,1)S(1)} %bitcast.22, bf16[1,256,16,128]{1,3,2,0:T(8,128)(2,1)} %bitcast.23), kind=kLoop, calls=%fused_computation | loop fusion | flops 1048576 | bytes 4194304 | tf_op jit(solution)/shard_map/transpose | solution.py:197
  19.9 3.9 %copy.19 = bf16[16,2,256,128]{3,2,1,0:T(8,128)(2,1)} copy(bf16[16,2,256,128]{2,3,0,1:T(8,128)(2,1)} %maximum_bitcast_fusion) | data formatting | bytes 4194304 | tf_op jit(solution)/shard_map/transpose | solution.py:197
  23.8 32.7 %all-to-all-done.1 = bf16[16,2,256,128]{3,2,1,0:T(8,128)(2,1)S(1)} async-done(((bf16[16,2,256,128]{3,2,1,0:T(8,128)(2,1)}), bf16[16,2,256,128]{3,2,1,0:T(8,128)(2,1)S(1)}, u32[]{:S(2)}, u32[]{:S(2)}) %all-to-all-start.1) | async-done | bytes 2097184 | tf_op jit(solution)/shard_map/all_to_all | solution.py:198
  56.5 9.2 %all-to-all-start = ((bf16[16,2,256,128]{3,2,1,0:T(8,128)(2,1)}), bf16[16,2,256,128]{3,2,1,0:T(8,128)(2,1)}, u32[]{:S(2)}, u32[]{:S(2)}) async-start(bf16[16,2,256,128]{3,2,1,0:T(8,128)(2,1)} %copy.19), calls=%async_computation | async-start | bytes 4194304 | tf_op jit(solution)/shard_map/all_to_all | solution.py:198
  65.7 0.0 copy-done
  65.7 0.1 dynamic-slice_bitcast_fusion.1.skip_ref
  65.8 0.8 dynamic-slice_bitcast_fusion.skip_ref
  66.5 0.0 copy-start.2
  66.5 0.0 copy-start.3
  66.5 0.1 fusion.1
  66.7 0.6 copy-done.2
  67.3 0.0 copy-done.3
  67.3 23.4 %shard_map.118.first_ref = f32[4096,128]{1,0:T(8,128)S(1)} custom-call(bf16[4096,128]{1,0:T(8,128)(2,1)S(1)} %bitcast.19, bf16[4096,128]{1,0:T(8,128)(2,1)S(1)} %bitcast.18, f32[1,128]{1,0:T(1,128)S(1)} %dynamic-slice_bitcast_fusion.1.skip_ref, bf16[64,144,64]{2,1,0:T(8,128)(2,1)} %constant.20.clone.forth, bf16[64,64,144]{2,1,0:T(8,128)(2,1)} %constant.21.clone.back, ...), custom_call_target="tpu_custom_call" | custom-call | flops 16000000000 | bytes 8000000 | tf_op jit(solution)/shard_map/pallas_call | solution.py:177
  90.7 18.2 %all-to-all-done = bf16[16,2,256,128]{3,2,1,0:T(8,128)(2,1)} async-done(((bf16[16,2,256,128]{3,2,1,0:T(8,128)(2,1)}), bf16[16,2,256,128]{3,2,1,0:T(8,128)(2,1)}, u32[]{:S(2)}, u32[]{:S(2)}) %all-to-all-start) | async-done | bytes 2097184 | tf_op jit(solution)/shard_map/all_to_all | solution.py:198
  109.0 1.8 fusion
  110.7 0.0 copy-start.1
  110.7 23.4 %shard_map.119.mixed_ref = bf16[4096,128]{1,0:T(8,128)(2,1)S(1)} custom-call(bf16[4096,128]{1,0:T(8,128)(2,1)S(1)} %bitcast.17, f32[4096,128]{1,0:T(8,128)S(1)} %shard_map.118.first_ref, bf16[4096,128]{1,0:T(8,128)(2,1)S(1)} %bitcast.16, f32[1,128]{1,0:T(1,128)S(1)} %dynamic-slice_bitcast_fusion.skip_ref, bf16[64,144,64]{2,1,0:T(8,128)(2,1)} %constant.20.clone.forth, ...), custom_call_target="tpu_custom_call" | custom-call | flops 16000000000 | bytes 8000000 | tf_op jit(solution)/shard_map/pallas_call | solution.py:177
  134.2 0.0 copy-done.1
  134.2 47.5 %shard_map.120 = bf16[256,2048]{1,0:T(8,128)(2,1)S(1)} custom-call(bf16[4096,128]{1,0:T(8,128)(2,1)S(1)} %shard_map.119.mixed_ref, bf16[256,2048]{1,0:T(8,128)(2,1)S(1)} %copy-done.1, bf16[2048,4096]{1,0:T(8,128)(2,1)} %weight_ref.1), custom_call_target="tpu_custom_call" | custom-call | flops 4294967296 | bytes 20000000 | tf_op jit(solution)/shard_map/pallas_call | solution.py:345
  181.7 1.0 copy.24
Async XLA Ops:
  0.0 65.7 %copy-start = (f32[2048]{0:T(1024)S(1)}, f32[2048]{0:T(1024)}, u32[]{:S(2)}) copy-start(f32[2048]{0:T(1024)} %param.17) | copy-start | bytes 24580
  0.0 1.6 copy-start.4
  6.7 49.8 %all-to-all-start.1 = ((bf16[16,2,256,128]{3,2,1,0:T(8,128)(2,1)}), bf16[16,2,256,128]{3,2,1,0:T(8,128)(2,1)S(1)}, u32[]{:S(2)}, u32[]{:S(2)}) async-start(bf16[16,2,256,128]{3,2,1,0:T(8,128)(2,1)} %copy.22), calls=%async_computation.1 | async-start | bytes 4194304 | tf_op jit(solution)/shard_map/all_to_all | solution.py:198
  56.5 52.4 %all-to-all-start = ((bf16[16,2,256,128]{3,2,1,0:T(8,128)(2,1)}), bf16[16,2,256,128]{3,2,1,0:T(8,128)(2,1)}, u32[]{:S(2)}, u32[]{:S(2)}) async-start(bf16[16,2,256,128]{3,2,1,0:T(8,128)(2,1)} %copy.19), calls=%async_computation | async-start | bytes 4194304 | tf_op jit(solution)/shard_map/all_to_all | solution.py:198
  66.5 0.8 copy-start.2
  66.5 0.8 copy-start.3
  110.7 23.4 %copy-start.1 = (bf16[256,2048]{1,0:T(8,128)(2,1)S(1)}, bf16[256,2048]{1,0:T(8,128)(2,1)}, u32[]{:S(2)}) copy-start(bf16[256,2048]{1,0:T(8,128)(2,1)} %gate_ref.1) | copy-start | bytes 3145732

commit v4 on v3

--- a/solution.py
+++ b/solution.py
@@ -100,44 +100,73 @@
     return tuple(jnp.asarray(t.astype(ml_dtypes.bfloat16)) for t in (forth, back, inside, inside.T))
 
 
-def convolve_rows(signal, taps, forth, back, inside, outside, signal_half, taps_half, total):
-    tokens, channels = signal.shape
-    half = tokens // INNER
+def widen(field):
+    return field.astype(jnp.float32)
+
+
+def outer_pass(pairs, forth):
+    half = pairs[0][0].shape[0] // INNER
     kept2 = forth.shape[1]
 
     def outer(b, _):
-        rows = pl.ds(b, half, stride=INNER)
-        both = jnp.concatenate([signal[rows, :], taps[rows, :]], axis=1).astype(jnp.bfloat16)
-        part = jnp.dot(forth[b], both, preferred_element_type=jnp.float32)
-        spread = pl.ds(b, kept2, stride=INNER)
-        signal_half[spread, :] = part[:, :channels]
-        taps_half[spread, :] = part[:, channels:]
+        rows, spread = pl.ds(b, half, stride=INNER), pl.ds(b, kept2, stride=INNER)
+        loaded = [source[rows, :] for source, _ in pairs]
+        both = jnp.concatenate(loaded, axis=1) if len(pairs) > 1 else loaded[0]
+        part = jnp.dot(forth[b], both.astype(jnp.bfloat16), preferred_element_type=jnp.float32)
+        width = loaded[0].shape[1]
+        for i, (_, result) in enumerate(pairs):
+            result[spread, :] = part[:, i * width : (i + 1) * width]
         return 0
 
     lax.fori_loop(0, INNER, outer, 0, unroll=4)
 
+
+def each_slab(half, body):
     group = math.gcd(half + 1, 5)
 
-    def inner(g, _):
-        slabs = [
-            pl.ds(pl.multiple_of((g * group + i) * 2 * INNER, 2 * INNER), 2 * INNER)
-            for i in range(group)
-        ]
-        sig = jnp.concatenate([signal_half[rows, :].astype(jnp.bfloat16) for rows in slabs], axis=1)
-        tap = jnp.concatenate([taps_half[rows, :].astype(jnp.bfloat16) for rows in slabs], axis=1)
-        sig = jnp.dot(inside[...], sig, preferred_element_type=jnp.float32)
-        tap = jnp.dot(inside[...], tap, preferred_element_type=jnp.float32)
+    def step(g, _):
+        body(
+            [
+                pl.ds(pl.multiple_of((g * group + i) * 2 * INNER, 2 * INNER), 2 * INNER)
+                for i in range(group)
+            ]
+        )
+        return 0
+
+    lax.fori_loop(0, (half + 1) // group, step, 0)
+
+
+def inner_spectrum(half_field, slabs, inside):
+    field = jnp.concatenate([half_field[rows, :].astype(jnp.bfloat16) for rows in slabs], axis=1)
+    return jnp.dot(inside[...], field, preferred_element_type=jnp.float32)
+
+
+def put_slabs(half_field, slabs, values):
+    channels = half_field.shape[1]
+    for i, rows in enumerate(slabs):
+        half_field[rows, :] = values[:, i * channels : (i + 1) * channels]
+
+
+def inner_pass(signal_half, taps_half, inside, outside, half, taps_done):
+    def body(slabs):
+        sig = inner_spectrum(signal_half, slabs, inside)
+        if taps_done:
+            tap = jnp.concatenate([taps_half[rows, :] for rows in slabs], axis=1)
+        else:
+            tap = inner_spectrum(taps_half, slabs, inside)
         sig_re, sig_im = sig[:INNER], sig[INNER:]
         tap_re, tap_im = tap[:INNER], tap[INNER:]
         product = jnp.concatenate(
             [sig_re * tap_re - sig_im * tap_im, sig_re * tap_im + sig_im * tap_re], axis=0
         ).astype(jnp.bfloat16)
         result = jnp.dot(outside[...], product, preferred_element_type=jnp.float32)
-        for i, rows in enumerate(slabs):
-            signal_half[rows, :] = result[:, i * channels : (i + 1) * channels]
-        return 0
-
-    lax.fori_loop(0, (half + 1) // group, inner, 0)
+        put_slabs(signal_half, slabs, result)
+
+    each_slab(half, body)
+
+
+def last_pass(signal_half, back, total):
+    half, kept2 = back.shape[1:]
 
     def last(b, _):
         folded = signal_half[pl.ds(b, kept2, stride=INNER), :].astype(jnp.bfloat16)
@@ -149,63 +178,146 @@
     lax.fori_loop(0, INNER, last, 0, unroll=4)
 
 
-def first_kernel(
-    taps_ref, value_ref, skip_ref, forth, back, inside, outside, out_ref,
-    signal, taps, signal_half, taps_half,
+def mixing_kernel(
+    count, taps_one_ref, value_ref, taps_two_ref, gate_ref, skip_one_ref, skip_two_ref,
+    forth_ref, back_ref, inside, outside, out_ref,
+    got, signal, taps, signal_half, taps_half, total, forth, back,
+    table_sem, local_sem, send_sem, recv_sem,
 ):
-    signal[...] = value_ref[...].astype(jnp.float32)
-    taps[...] = taps_ref[...].astype(jnp.float32)
-    convolve_rows(signal, taps, forth, back, inside, outside, signal_half, taps_half, out_ref)
-    out_ref[...] += skip_ref[...] * signal[...]
-
-
-def second_kernel(
-    taps_ref, first_ref, gate_ref, skip_ref, forth, back, inside, outside, out_ref,
-    signal, taps, signal_half, taps_half, total,
-):
-    mixed = (gate_ref[...].astype(jnp.float32) * first_ref[...]).astype(jnp.bfloat16)
-    signal[...] = mixed.astype(jnp.float32)
-    taps[...] = taps_ref[...].astype(jnp.float32)
-    convolve_rows(signal, taps, forth, back, inside, outside, signal_half, taps_half, total)
-    out_ref[...] = (total[...] + skip_ref[...] * signal[...]).astype(jnp.bfloat16)
-
-
-def call_local(kernel, dtype, tokens, channels, extra, *operands):
-    kept2 = operands[-4].shape[1]
-    field = pltpu.VMEM((tokens, channels), jnp.float32)
-    half_field = pltpu.VMEM((kept2 * INNER, channels), jnp.float32)
-    return pl.pallas_call(
-        kernel,
-        out_shape=jax.ShapeDtypeStruct((tokens, channels), dtype),
-        in_specs=[pl.BlockSpec(memory_space=pltpu.VMEM)] * len(operands),
-        out_specs=pl.BlockSpec(memory_space=pltpu.VMEM),
-        scratch_shapes=[field, field, half_field, half_field] + [field] * extra,
-        compiler_params=pltpu.CompilerParams(vmem_limit_bytes=48 * 1024 * 1024),
-        cost_estimate=pl.CostEstimate(
-            flops=16_000_000_000, bytes_accessed=8_000_000, transcendentals=0
-        ),
-    )(*operands)
+    me, side = lax.axis_index("seq"), lax.axis_index("ch")
+    tok_rows, channels = value_ref.shape
+    share = channels // count
+    half = forth_ref.shape[2]
+    stride = max(count // 2 - 1, 1)
+    fields = (taps_one_ref, value_ref, taps_two_ref, gate_ref)
+
+    forth_copy = pltpu.make_async_copy(forth_ref, forth, table_sem.at[0])
+    back_copy = pltpu.make_async_copy(back_ref, back, table_sem.at[1])
+
+    barrier = pltpu.get_barrier_semaphore()
+
+    def greet(j, _):
+        pl.semaphore_signal(barrier, inc=1, device_id=(lax.rem(me + j, count), side))
+        return 0
+
+    lax.fori_loop(1, count, greet, 0)
+    pl.semaphore_wait(barrier, count - 1)
+
+    def columns_of(owner):
+        return pl.ds(pl.multiple_of(owner * share, share), share)
+
+    def rows_of(owner):
+        return pl.ds(pl.multiple_of(owner * tok_rows, tok_rows), tok_rows)
+
+    def field_copy(f, j, target, owner):
+        return pltpu.make_async_remote_copy(
+            src_ref=fields[f].at[:, columns_of(target)],
+            dst_ref=got.at[f, rows_of(owner), :],
+            send_sem=send_sem.at[f, j],
+            recv_sem=recv_sem.at[f, j],
+            device_id=(target, side),
+        )
+
+    def local_copy(f):
+        return pltpu.make_async_copy(
+            fields[f].at[:, columns_of(me)], got.at[f, rows_of(me), :], local_sem.at[f]
+        )
+
+    def send(f):
+        def one(i, _):
+            j = 1 + lax.rem(stride * (i + 1), count - 1)
+            field_copy(f, j, lax.rem(me + j, count), me).start()
+            return 0
+
+        lax.fori_loop(0, count - 1, one, 0)
+        local_copy(f).start()
+
+    def receive(f):
+        def one(j, _):
+            field_copy(f, j, lax.rem(me + j, count), lax.rem(me + count - j, count)).wait_recv()
+            return 0
+
+        lax.fori_loop(1, count, one, 0)
+        local_copy(f).wait()
+
+    send(0)
+    send(1)
+    forth_copy.start()
+    back_copy.start()
+    receive(0)
+    send(2)
+    taps[...] = widen(got[0])
+    receive(1)
+    send(3)
+    signal[...] = widen(got[1])
+    forth_copy.wait()
+    back_copy.wait()
+    outer_pass([(signal, signal_half), (taps, taps_half)], forth)
+    inner_pass(signal_half, taps_half, inside, outside, half, False)
+    last_pass(signal_half, back, total)
+    total[...] += skip_one_ref[...] * signal[...]
+
+    receive(2)
+    taps[...] = widen(got[2])
+    outer_pass([(taps, taps_half)], forth)
+    each_slab(
+        half, lambda slabs: put_slabs(taps_half, slabs, inner_spectrum(taps_half, slabs, inside))
+    )
+
+    receive(3)
+    signal[...] = widen((widen(got[3]) * total[...]).astype(jnp.bfloat16))
+    outer_pass([(signal, signal_half)], forth)
+    inner_pass(signal_half, taps_half, inside, outside, half, True)
+    last_pass(signal_half, back, total)
+    out_ref[...] = (total[...] + skip_two_ref[...] * signal[...]).astype(jnp.bfloat16)
+
+    for f in range(len(fields)):
+
+        def sent(j, _):
+            field_copy(f, j, lax.rem(me + j, count), me).wait_send()
+            return 0
+
+        lax.fori_loop(1, count, sent, 0)
 
 
 def local_mixing(first_filter, value_stream, first_gate, second_filter, skip_one, skip_two):
     rows, channels = value_stream.shape
-    seq_count = lax.axis_size("seq")
-    tokens, share = rows * seq_count, channels // seq_count
-    tables = folded_tables(tokens)
-
-    def pair(one, two):
-        both = jnp.stack([one, two]).reshape(2, rows, seq_count, share).transpose(2, 0, 1, 3)
-        got = lax.all_to_all(both, "seq", split_axis=0, concat_axis=0, tiled=True)
-        return got[:, 0].reshape(tokens, share), got[:, 1].reshape(tokens, share)
-
-    taps_one, value = pair(first_filter, value_stream)
-    gate_one, taps_two = pair(first_gate, second_filter)
-    first = call_local(
-        first_kernel, jnp.float32, tokens, share, 0, taps_one, value, skip_one[None, :], *tables
-    )
-    return call_local(
-        second_kernel, jnp.bfloat16, tokens, share, 1,
-        taps_two, first, gate_one, skip_two[None, :], *tables,
+    count = lax.axis_size("seq")
+    tokens, share = rows * count, channels // count
+    forth, back, inside, outside = folded_tables(tokens)
+    in_vmem = pl.BlockSpec(memory_space=pltpu.VMEM)
+    anywhere = pl.BlockSpec(memory_space=pl.ANY)
+    dma = pltpu.SemaphoreType.DMA
+    field = pltpu.VMEM((tokens, share), jnp.float32)
+    half_field = pltpu.VMEM((forth.shape[1] * INNER, share), jnp.float32)
+    return pl.pallas_call(
+        functools.partial(mixing_kernel, count),
+        out_shape=jax.ShapeDtypeStruct((tokens, share), jnp.bfloat16),
+        in_specs=[anywhere] * 4 + [in_vmem] * 2 + [anywhere] * 2 + [in_vmem] * 2,
+        out_specs=in_vmem,
+        scratch_shapes=[
+            pltpu.VMEM((4, tokens, share), jnp.bfloat16),
+            field,
+            field,
+            half_field,
+            half_field,
+            field,
+            pltpu.VMEM(forth.shape, jnp.bfloat16),
+            pltpu.VMEM(back.shape, jnp.bfloat16),
+            dma((2,)),
+            dma((4,)),
+            dma((4, count)),
+            dma((4, count)),
+        ],
+        compiler_params=pltpu.CompilerParams(
+            collective_id=1, has_side_effects=True, vmem_limit_bytes=48 * 1024 * 1024
+        ),
+        cost_estimate=pl.CostEstimate(
+            flops=20_000_000_000, bytes_accessed=16_000_000, transcendentals=0
+        ),
+    )(
+        first_filter, value_stream, second_filter, first_gate,
+        skip_one[None, :], skip_two[None, :], forth, back, inside, outside,
     )
 
 
@@ -281,7 +393,7 @@
         local_copy(q).start()
         return 0
 
-    lax.fori_loop(0, CHUNKS, send_chunk, 0)
+    lax.fori_loop(0, 2, send_chunk, 0)
     weight_copy(0, 1 - side).wait()
     weight_copy(1, side).wait()
 
@@ -292,6 +404,11 @@
 
         lax.fori_loop(1, count, receive, 0)
         local_copy(q).wait()
+
+        @pl.when(q + 2 < CHUNKS)
+        def _():
+            send_chunk(q + 2, 0)
+
         gate_rows = pl.ds(pl.multiple_of(q * piece, piece), piece)
         gated[...] = (
             gate_ref[gate_rows, :].astype(jnp.float32) * rows[q].astype(jnp.float32)

time: 183 us -> 166 us (0.907)
  Pallas kernels: 94.4 us -> 157 us
  waiting for transfers between devices: 51 us -> 0 us
  starting transfers between devices: 15.8 us -> 0 us
  local copies, waits for them, and re-layouts: 17.3 us -> 8.17 us
  other arithmetic: 4.16 us -> 0 us
    pallas_call x2 -> x1, Pallas kernels: 46.9 us -> 113 us  [local_mixing(): pl.pallas_call(functools.partial(mixing_kernel, count), out_shape=jax.Sha...]
    all_to_all x2 -> x0, waiting for transfers between devices: 51 us -> none  [pair(): got = lax.all_to_all(both, 'seq', split_axis=0, concat_axis=0, tiled=True)]
    all_to_all x2 -> x0, starting transfers between devices: 15.8 us -> none  [pair(): got = lax.all_to_all(both, 'seq', split_axis=0, concat_axis=0, tiled=True)]
    transpose x2 -> x0, local copies, waits for them, and re-layouts: 6.32 us -> none  [pair(): jnp.stack([one, two]).reshape(2, rows, seq_count, share)]
    pallas_call x1, Pallas kernels: 47.5 us -> 43.2 us  [project_rows(): pl.pallas_call(functools.partial(tail_kernel, count), out_shape=jax.Shape...]
    transpose x2 -> x0, other arithmetic: 4.16 us -> none  [pair(): jnp.stack([one, two]).reshape(2, rows, seq_count, share)]
    slice x2 -> x0, local copies, waits for them, and re-layouts: 1.89 us -> none  [pair(): return (got[:, 0].reshape(tokens, share), got[:, 1].reshape(tokens, share))]
  transfers between devices with their start and end apart: 2 -> 0, of which waited for: 2 -> 0; matrix products, arithmetic and copies ran while one was open for 6% -> 0% of each run, Pallas kernels for 13% -> 0%
where the time goes in v4:
time: 166 us; the launch traced here: 165 us
  Pallas kernels  157 us (95%)
  local copies, waits for them, and re-layouts  8.17 us (5%)
    pallas_call x1, Pallas kernels, local_mixing(): pl.pallas_call(functools.partial(mixing_kernel, count), out_shape=jax.Sha...  113 us
    pallas_call x1, Pallas kernels, project_rows(): pl.pallas_call(functools.partial(tail_kernel, count), out_shape=jax.Shape...  43.2 us
    unnamed x15, local copies, waits for them, and re-layouts  7.39 us

profile of v4, /device:TPU:5, one launch (start us, length us, event | category | flops | bytes accessed | tf_op | source)
XLA Modules:
  0.0 164.8 jit_solution(9549860652913996134)
XLA Ops:
  0.0 0.8 dynamic-slice_bitcast_fusion
  0.8 0.0 copy-start.1
  0.8 1.2 copy-done.1
  2.0 0.0 copy-start.2
  2.0 1.2 copy-done.2
  3.2 0.0 copy-start.3
  3.2 1.2 copy-done.3
  4.5 0.0 copy-start.4
  4.5 1.2 copy-done.4
  5.7 0.0 copy-start.5
  5.7 0.8 copy-done.5
  6.4 0.0 copy-start.6
  6.4 0.8 copy-done.6
  7.2 0.0 copy-start
  7.2 113.4 %shard_map.118.mixed_ref = bf16[4096,128]{1,0:T(8,128)(2,1)S(1)} custom-call(bf16[256,2048]{1,0:T(8,128)(2,1)S(1)} %copy-done.1, bf16[256,2048]{1,0:T(8,128)(2,1)S(1)} %copy-done.2, bf16[256,2048]{1,0:T(8,128)(2,1)S(1)} %copy-done.3, bf16[256,2048]{1,0:T(8,128)(2,1)S(1)} %copy-done.4, f32[1,128]{1,0:T(1,128)S(1)} %get-tuple-element.6.skip_one_ref, ...), custom_call_target="tpu_custom_call" | custom-call | flops 20000000000 | bytes 16000000 | tf_op jit(solution)/shard_map/pallas_call | solution.py:293
  120.6 0.0 copy-done
  120.7 43.2 %shard_map.119 = bf16[256,2048]{1,0:T(8,128)(2,1)S(1)} custom-call(bf16[4096,128]{1,0:T(8,128)(2,1)S(1)} %shard_map.118.mixed_ref, bf16[256,2048]{1,0:T(8,128)(2,1)S(1)} %copy-done, bf16[2048,4096]{1,0:T(8,128)(2,1)} %weight_ref.1), custom_call_target="tpu_custom_call" | custom-call | flops 4294967296 | bytes 20000000 | tf_op jit(solution)/shard_map/pallas_call | solution.py:462
  163.8 1.0 copy.14
Async XLA Ops:
  0.8 1.2 copy-start.1
  2.0 1.2 copy-start.2
  3.2 1.2 copy-start.3
  4.5 1.2 copy-start.4
  5.7 0.8 copy-start.5
  6.4 0.8 copy-start.6
  7.2 113.5 %copy-start = (bf16[256,2048]{1,0:T(8,128)(2,1)S(1)}, bf16[256,2048]{1,0:T(8,128)(2,1)}, u32[]{:S(2)}) copy-start(bf16[256,2048]{1,0:T(8,128)(2,1)} %gate_ref.3) | copy-start | bytes 3145732

commit v5 on v4

--- a/solution.py
+++ b/solution.py
@@ -310,7 +310,7 @@
             dma((4, count)),
         ],
         compiler_params=pltpu.CompilerParams(
-            collective_id=1, has_side_effects=True, vmem_limit_bytes=48 * 1024 * 1024
+            collective_id=1, has_side_effects=True, vmem_limit_bytes=60 * 1024 * 1024
         ),
         cost_estimate=pl.CostEstimate(
             flops=20_000_000_000, bytes_accessed=16_000_000, transcendentals=0
@@ -321,7 +321,7 @@
     )
 
 
-CHUNKS = 4
+CHUNKS = 2
 TILE = 512
 
 
@@ -368,12 +368,13 @@
             device_id=(target, side),
         )
 
-    def side_copy(q):
+    def side_copy(q, t):
+        columns = pl.ds(pl.multiple_of(t * TILE, TILE), TILE)
         return pltpu.make_async_remote_copy(
-            src_ref=theirs.at[q],
-            dst_ref=arrived.at[q],
-            send_sem=side_send.at[q],
-            recv_sem=side_recv.at[q],
+            src_ref=theirs.at[q, :, columns],
+            dst_ref=arrived.at[q, :, columns],
+            send_sem=side_send.at[q, t],
+            recv_sem=side_recv.at[q, t],
             device_id=(me, 1 - side),
         )
 
@@ -393,7 +394,7 @@
         local_copy(q).start()
         return 0
 
-    lax.fori_loop(0, 2, send_chunk, 0)
+    lax.fori_loop(0, CHUNKS, send_chunk, 0)
     weight_copy(0, 1 - side).wait()
     weight_copy(1, side).wait()
 
@@ -404,10 +405,6 @@
 
         lax.fori_loop(1, count, receive, 0)
         local_copy(q).wait()
-
-        @pl.when(q + 2 < CHUNKS)
-        def _():
-            send_chunk(q + 2, 0)
 
         gate_rows = pl.ds(pl.multiple_of(q * piece, piece), piece)
         gated[...] = (
@@ -423,6 +420,7 @@
         def for_other(t, _):
             columns, terms = project(0, t)
             theirs[q, :, columns] = terms.astype(jnp.bfloat16)
+            side_copy(q, t).start()
             return 0
 
         def for_self(t, _):
@@ -431,17 +429,24 @@
             return 0
 
         lax.fori_loop(0, width // TILE, for_other, 0)
-        side_copy(q).start()
         lax.fori_loop(0, width // TILE, for_self, 0)
         return 0
 
     lax.fori_loop(0, CHUNKS, work, 0)
 
     def finish(q, _):
-        side_copy(q).wait_recv()
         out_rows = pl.ds(pl.multiple_of(q * piece, piece), piece)
-        out_ref[out_rows, :] = (own[q] + arrived[q].astype(jnp.float32)).astype(jnp.bfloat16)
-        side_copy(q).wait_send()
+
+        def add(t, _):
+            side_copy(q, t).wait_recv()
+            columns = pl.ds(pl.multiple_of(t * TILE, TILE), TILE)
+            out_ref[out_rows, columns] = (
+                own[q, :, columns] + arrived[q, :, columns].astype(jnp.float32)
+            ).astype(jnp.bfloat16)
+            side_copy(q, t).wait_send()
+            return 0
+
+        lax.fori_loop(0, width // TILE, add, 0)
 
         def sent(j, _):
             row_copy(q, j, lax.rem(me + j, count), me).wait_send()
@@ -475,8 +480,8 @@
             dma((CHUNKS,)),
             dma((CHUNKS, count)),
             dma((CHUNKS, count)),
-            dma((CHUNKS,)),
-            dma((CHUNKS,)),
+            dma((CHUNKS, width // TILE)),
+            dma((CHUNKS, width // TILE)),
         ],
         compiler_params=pltpu.CompilerParams(
             collective_id=0, has_side_effects=True, vmem_limit_bytes=48 * 1024 * 1024

time: 166 us -> 167 us (level)
  Pallas kernels: 157 us -> 163 us
  local copies, waits for them, and re-layouts: 8.17 us -> 3.55 us
    unnamed x15 -> x5, local copies, waits for them, and re-layouts: 7.39 us -> 2.19 us
    pallas_call x1, Pallas kernels: 43.2 us -> 47.7 us  [project_rows(): pl.pallas_call(functools.partial(tail_kernel, count), out_shape=jax.Shape...]
    pallas_call x1, Pallas kernels: 113 us -> 116 us  [local_mixing(): pl.pallas_call(functools.partial(mixing_kernel, count), out_shape=jax.Sha...]
where the time goes in v5:
time: 167 us
  Pallas kernels  163 us (98%)
  local copies, waits for them, and re-layouts  3.55 us (2%)
    pallas_call x1, Pallas kernels, local_mixing(): pl.pallas_call(functools.partial(mixing_kernel, count), out_shape=jax.Sha...  116 us
    pallas_call x1, Pallas kernels, project_rows(): pl.pallas_call(functools.partial(tail_kernel, count), out_shape=jax.Shape...  47.7 us

profile of v5, /device:TPU:5, one launch (start us, length us, event | category | flops | bytes accessed | tf_op | source)
XLA Modules:
  0.0 166.8 jit_solution(14237496014918694455)
XLA Ops:
  0.0 1.4 dynamic-slice_bitcast_fusion
  1.4 0.0 copy-start
  1.4 115.5 %shard_map.118.mixed_ref = bf16[4096,128]{1,0:T(8,128)(2,1)} custom-call(bf16[256,2048]{1,0:T(8,128)(2,1)} %taps_one_ref.1, bf16[256,2048]{1,0:T(8,128)(2,1)} %value_ref.1, bf16[256,2048]{1,0:T(8,128)(2,1)} %taps_two_ref.1, bf16[256,2048]{1,0:T(8,128)(2,1)} %gate_ref.2, f32[1,128]{1,0:T(1,128)} %get-tuple-element.6.skip_one_ref, ...), custom_call_target="tpu_custom_call" | custom-call | flops 20000000000 | bytes 16000000 | tf_op jit(solution)/shard_map/pallas_call | solution.py:293
  116.9 0.0 copy-done
  116.9 0.0 copy-start.1
  116.9 1.2 copy-done.1
  118.1 47.7 %shard_map.119 = bf16[256,2048]{1,0:T(8,128)(2,1)S(1)} custom-call(bf16[4096,128]{1,0:T(8,128)(2,1)S(1)} %copy-done.1, bf16[256,2048]{1,0:T(8,128)(2,1)S(1)} %copy-done, bf16[2048,4096]{1,0:T(8,128)(2,1)} %weight_ref.1), custom_call_target="tpu_custom_call" | custom-call | flops 4294967296 | bytes 20000000 | tf_op jit(solution)/shard_map/pallas_call | solution.py:467
  165.8 1.0 copy.14
Async XLA Ops:
  1.4 115.5 %copy-start = (bf16[256,2048]{1,0:T(8,128)(2,1)S(1)}, bf16[256,2048]{1,0:T(8,128)(2,1)}, u32[]{:S(2)}) copy-start(bf16[256,2048]{1,0:T(8,128)(2,1)} %gate_ref.3) | copy-start | bytes 3145732
  116.9 1.2 copy-start.1
